TPU v7x, 512 devices: a whole 4x4x16 slice. The times are simulated.
512 devices in a mesh: tp: 8 (over x, core), dp: 64 (over z, y).
Axes of the slice: x: 4, y: 4, z: 16, core: 2. Of those that a mesh axis runs over, the one named last changes fastest.
Arguments:
- queries: bfloat16 [256, 128, 576], P('dp'), may hold values from -30 to 30
- lengths: int32 [256], P('dp'), may hold values from 2 to 1024, as said below
- resident_pages: bfloat16 [2048, 64, 576], P('dp', 'tp'), may hold values from -3 to 3
- resident_scale: bfloat16 [2048], P('dp'), may hold values from 0.69921875 to 1.34375
- prefill_written_pages: bfloat16 [2048, 64, 576], P('dp', 'tp'), may hold values from -3 to 3
- prefill_scale: bfloat16 [2048], P('dp'), may hold values from 0.69921875 to 1.34375
- page_slot: int32 [2048], P('dp'), may hold values from 0 to 2047, as said below
- tokens: bfloat16 [1024, 7168], P('dp'), may hold values from -3 to 3
- expert_ids: int32 [1024, 8], P('dp'), may hold values from 0 to 31, all different within a row; in each aligned block of 16 rows (0 to 15, 16 to 31, ...) at most 8 rows name the same one
- gate_weights: bfloat16 [1024, 8], P('dp'), may hold values from 0.079589844 to 0.29882812
- gate_projection: bfloat16 [64, 7168, 512], P('dp', 'tp'), may hold values from -0.0625 to 0.0625
- up_weights: bfloat16 [64, 7168, 512], P('dp', 'tp'), may hold values from -0.0625 to 0.0625
- down_weights: bfloat16 [64, 512, 7168], P('dp', None, 'tp'), may hold values from -0.1875 to 0.1875
Outputs:
- attention_out: bfloat16 [256, 128, 512], P('dp', 'tp')
- moe_out: bfloat16 [1024, 7168], P('dp', 'tp')
Inputs may be any that keep to these rules, and one draw needn't show every extreme that they name: `page_slot`: A permutation of the slots. Slot s is position s % 32 of dp index s // 32. Of the pages held by one dp index at most 1 go to any one dp index, and every dp index sends its pages with the same multiset of offsets (target index minus own index, modulo 64). `lengths`: some request has exactly 1024. `expert_ids`: of the rows of one dp index, at most 8 name any one expert.
All inputs are finite; a program needn't handle non-finite values.
Results may differ from a plain program's by a relative error of at most 0.0065.
Values may be sent and summed in bfloat16 or wider, within the bound.
A program may use at most 64 MiB of HBM per device.

v0:
```python
import jax
import jax.numpy as jnp
from jax import lax
from jax.sharding import PartitionSpec as P

LATENT_WIDTH = 512


softmax_factor = 192.0 ** (-0.5)
masked_score = -1e30


def combined_all(value, axis, join):
    pieces = jax.tree.map(lambda part: lax.all_gather(part, axis), value)
    head = jax.tree.map(lambda part: part[0], pieces)
    tail = jax.tree.map(lambda part: part[1:], pieces)
    running, _ = lax.scan(lambda running, slab: (join(running, slab), None), head, tail)
    return running


def fold_softmax(left, right):
    left_max, left_total, left_acc = left
    right_max, right_total, right_acc = right
    highest = jnp.maximum(left_max, right_max)
    left_factor = jnp.exp(left_max - highest)
    right_factor = jnp.exp(right_max - highest)
    return (
        highest,
        left_total * left_factor + right_total * right_factor,
        left_acc * left_factor[..., None] + right_acc * right_factor[..., None],
    )


def exclusive_ranks(labels, count):
    onehot = (labels[:, None] == jnp.arange(count)[None, :]).astype(jnp.int32)
    return jnp.sum((jnp.cumsum(onehot, axis=0) - onehot) * onehot, axis=1)


def attend_local(queries, latent_rows, token_scales, lengths, tp_index, per_page, n_tp):
    row_count = latent_rows.shape[1]
    local_rows = jnp.arange(row_count)
    position = (
        local_rows // per_page * (per_page * n_tp) + tp_index * per_page + local_rows % per_page
    )
    visible = position[None, None, :] < lengths[:, None, None]
    scores = jnp.einsum("bhc,btc->bht", queries, latent_rows, preferred_element_type=jnp.float32)
    scores = scores * (token_scales * softmax_factor)[:, None, :]
    scores = jnp.where(visible, scores, masked_score)
    highest = jnp.max(scores, axis=2)
    expos = jnp.where(visible, jnp.exp(scores - highest[..., None]), 0.0)
    denominator = jnp.sum(expos, axis=2)
    weight_rows = (expos * token_scales[:, None, :]).astype(jnp.bfloat16)
    summed_rows = jnp.einsum(
        "kyz,kzp->kyp",
        weight_rows,
        latent_rows[:, :, :LATENT_WIDTH],
        preferred_element_type=jnp.float32,
    )
    return (highest, denominator, summed_rows)


def on_device(
    queries,
    lengths,
    resident_pages,
    resident_scale,
    prefill_written_pages,
    prefill_scale,
    page_slot,
    tokens,
    expert_ids,
    gate_weights,
    gate_projection,
    up_weights,
    down_weights,
):
    n_dp = lax.axis_size("dp")
    n_tp = lax.axis_size("tp")
    tp_index = lax.axis_index("tp")
    per_source, per_page, key_value_width = prefill_written_pages.shape
    page_capacity = (per_source + n_dp - 1) // n_dp
    target_owner = page_slot // per_source
    position = page_slot % per_source
    send_slot = target_owner * page_capacity + exclusive_ranks(target_owner, n_dp)
    placing = send_slot[:, None] == jnp.arange(n_dp * page_capacity)[None, :]
    placing_matrix = placing.astype(jnp.bfloat16)
    sent_pages = jnp.dot(
        placing_matrix.T,
        prefill_written_pages.reshape(per_source, per_page * key_value_width),
        preferred_element_type=jnp.float32,
    ).astype(jnp.bfloat16)
    sent_scales = jnp.dot(
        placing_matrix.T, prefill_scale[:, None], preferred_element_type=jnp.float32
    )[:, 0].astype(jnp.bfloat16)
    sent_position = jnp.max(jnp.where(placing, position[:, None], -1), axis=0)
    got_pages, got_position, got_scales = (
        lax.all_to_all(
            sent_pages.reshape(n_dp, page_capacity, per_page * key_value_width),
            "dp",
            split_axis=0,
            concat_axis=0,
            tiled=True,
        ),
        lax.all_to_all(
            sent_position.reshape(n_dp, page_capacity),
            "dp",
            split_axis=0,
            concat_axis=0,
            tiled=True,
        ),
        lax.all_to_all(
            sent_scales.reshape(n_dp, page_capacity), "dp", split_axis=0, concat_axis=0, tiled=True
        ),
    )
    taking = (jnp.arange(per_source)[:, None] == got_position.reshape(-1)[None, :]).astype(
        jnp.bfloat16
    )
    new_pages = jnp.dot(
        taking,
        got_pages.reshape(n_dp * page_capacity, per_page * key_value_width),
        preferred_element_type=jnp.float32,
    ).astype(jnp.bfloat16)
    new_scales = jnp.dot(taking, got_scales, preferred_element_type=jnp.float32)[:, 0]
    requests = queries.shape[0]
    kind = requests // 2
    page_count = per_source // kind
    latent_rows = jnp.concatenate(
        [
            resident_pages.reshape(kind, page_count * per_page, key_value_width),
            new_pages.reshape(kind, page_count * per_page, key_value_width),
        ],
        axis=0,
    )
    page_scales = jnp.concatenate(
        [
            resident_scale.astype(jnp.float32).reshape(kind, page_count),
            new_scales.reshape(kind, page_count),
        ],
        axis=0,
    )
    token_scales = jnp.repeat(page_scales, per_page, axis=1)
    highest, denominator, summed_rows = attend_local(
        queries, latent_rows, token_scales, lengths, tp_index, per_page, n_tp
    )
    heads_dev = queries.shape[1] // n_tp
    highest, denominator, summed_rows = combined_all(
        (highest, denominator, summed_rows), "tp", fold_softmax
    )
    head_start = tp_index * heads_dev
    denominator = lax.dynamic_slice_in_dim(denominator, head_start, heads_dev, 1)
    summed_rows = lax.dynamic_slice_in_dim(summed_rows, head_start, heads_dev, 1)
    attention_out = (summed_rows / denominator[..., None]).astype(jnp.bfloat16)
    tok_dev, top_count = expert_ids.shape
    n_experts = n_dp // 2
    capacity = max(2, min(tok_dev, 2 * tok_dev * top_count // n_experts))
    width = tokens.shape[1]
    width_dev = width // n_tp
    picks = tok_dev * top_count
    flat_ids = expert_ids.reshape(-1)
    pick_slot = flat_ids * capacity + exclusive_ranks(flat_ids, n_experts)
    slot_hits = (pick_slot[:, None] == jnp.arange(n_experts * capacity)[None, :]).astype(
        jnp.float32
    )
    owner_rows = ((jnp.arange(picks) // top_count)[:, None] == jnp.arange(tok_dev)[None, :]).astype(
        jnp.float32
    )
    gather_expert = jnp.dot(slot_hits.T, owner_rows, precision=lax.Precision.HIGHEST)
    gathering = (
        jnp.broadcast_to(
            gather_expert.reshape(n_experts, 1, capacity, tok_dev),
            (n_experts, 2, capacity, tok_dev),
        )
        .reshape(n_dp * capacity, tok_dev)
        .astype(jnp.bfloat16)
    )
    combine_expert = jnp.dot(
        owner_rows.T,
        slot_hits * gate_weights.reshape(-1)[:, None].astype(jnp.float32),
        precision=lax.Precision.HIGHEST,
    )
    combining = (
        jnp.broadcast_to(
            combine_expert.reshape(tok_dev, n_experts, 1, capacity),
            (tok_dev, n_experts, 2, capacity),
        )
        .reshape(tok_dev, n_dp * capacity)
        .astype(jnp.bfloat16)
    )
    gate_local = gate_projection[0]
    up_local = up_weights[0]
    down_local = down_weights[0]
    own_columns = lax.dynamic_slice_in_dim(tokens, tp_index * width_dev, width_dev, 1)
    outgoing = (
        jnp.dot(gathering, own_columns, preferred_element_type=jnp.float32)
        .astype(jnp.bfloat16)
        .reshape(n_dp, capacity, width_dev)
    )
    arrived_rows = lax.all_to_all(outgoing, "dp", split_axis=0, concat_axis=0, tiled=True)
    item_count = arrived_rows.shape[1]
    flat_rows = arrived_rows.reshape(n_dp * item_count, width_dev)
    gate_part = jnp.dot(flat_rows, gate_local, preferred_element_type=jnp.float32)
    up_part = jnp.dot(flat_rows, up_local, preferred_element_type=jnp.float32)
    gate_sum, up_sum = lax.psum((gate_part, up_part), "tp")
    hidden = (jax.nn.silu(gate_sum) * up_sum).astype(jnp.bfloat16)
    result = jnp.dot(hidden, down_local, preferred_element_type=jnp.float32).astype(jnp.bfloat16)
    outputs = result.reshape(n_dp, item_count, width_dev)
    returned = lax.all_to_all(outputs, "dp", split_axis=0, concat_axis=0, tiled=True).reshape(
        n_dp * capacity, width_dev
    )
    moe_out = jnp.dot(combining, returned, preferred_element_type=jnp.float32).astype(jnp.bfloat16)
    return (attention_out, moe_out)


def solution(mesh):
    placed = (
        P("dp", None, None),
        P("dp"),
        P("dp", "tp", None),
        P("dp"),
        P("dp", "tp", None),
        P("dp"),
        P("dp"),
        P("dp", None),
        P("dp", None),
        P("dp", None),
        P("dp", "tp", None),
        P("dp", "tp", None),
        P("dp", None, "tp"),
    )
    return jax.shard_map(
        on_device,
        mesh=mesh,
        in_specs=placed,
        out_specs=(P("dp", "tp", None), P("dp", "tp")),
        check_vma=False,
    )
```

profile of v0, /device:TPU:7, one launch (start us, length us, event | category | flops | bytes accessed | tf_op | source)
XLA Modules:
  0.0 305.6 jit_solution(15386153567802202022)
XLA Ops:
  7.2 0.7 and_select_fusion
  8.2 0.8 fusion.9
  9.1 0.7 copy.55
  9.8 18.4 %all-to-all-start.2 = ((bf16[64,1,1]{2,1,0:T(2,128)(2,1)}), bf16[64,1,1]{2,1,0:T(2,128)(2,1)S(1)}, u32[]{:S(2)}, u32[]{:S(2)}) async-start(bf16[64,1,1]{2,1,0:T(2,128)(2,1)} %copy.55), calls=%async_computation.2 | async-start | bytes 65536 | tf_op jit(solution)/shard_map/all_to_all | solution.py:111
  28.4 0.7 copy.51
  29.1 0.8 copy.58
  30.4 0.3 convolution_convert_fusion.5
  30.8 11.1 %all-to-all-done.2 = bf16[64,1,1]{2,1,0:T(2,128)(2,1)S(1)} async-done(((bf16[64,1,1]{2,1,0:T(2,128)(2,1)}), bf16[64,1,1]{2,1,0:T(2,128)(2,1)S(1)}, u32[]{:S(2)}, u32[]{:S(2)}) %all-to-all-start.2) | async-done | bytes 160 | tf_op jit(solution)/shard_map/all_to_all | solution.py:111
  41.9 4.6 %all-to-all-start = ((s32[64,1,1]{2,1,0:T(1,128)}), s32[64,1,1]{2,1,0:T(1,128)S(1)}, u32[]{:S(2)}, u32[]{:S(2)}) async-start(s32[64,1,1]{2,1,0:T(1,128)} %copy.51), calls=%async_computation | async-start | bytes 65536 | tf_op jit(solution)/shard_map/all_to_all | solution.py:104
  46.5 2.0 fusion.4
  48.6 11.4 %all-to-all-done = s32[64,1,1]{2,1,0:T(1,128)S(1)} async-done(((s32[64,1,1]{2,1,0:T(1,128)}), s32[64,1,1]{2,1,0:T(1,128)S(1)}, u32[]{:S(2)}, u32[]{:S(2)}) %all-to-all-start) | async-done | bytes 288 | tf_op jit(solution)/shard_map/all_to_all | solution.py:104
  60.0 4.6 %all-to-all-start.3 = ((bf16[64,8,896]{2,1,0:T(8,128)(2,1)}), bf16[64,8,896]{2,1,0:T(8,128)(2,1)S(1)}, u32[]{:S(2)}, u32[]{:S(2)}) async-start(bf16[64,8,896]{2,1,0:T(8,128)(2,1)} %fusion.4), calls=%async_computation.3 | async-start | bytes 1835008 | tf_op jit(solution)/shard_map/all_to_all | solution.py:198
  64.7 0.2 reshape.190
  64.9 0.4 fusion.3
  65.4 0.5 broadcast.185
  65.9 1.1 reduce.2
  66.9 1.0 reshape.235
  67.9 39.8 %all-to-all-done.3 = bf16[64,8,896]{2,1,0:T(8,128)(2,1)S(1)} async-done(((bf16[64,8,896]{2,1,0:T(8,128)(2,1)}), bf16[64,8,896]{2,1,0:T(8,128)(2,1)S(1)}, u32[]{:S(2)}, u32[]{:S(2)}) %all-to-all-start.3) | async-done | bytes 917536 | tf_op jit(solution)/shard_map/all_to_all | solution.py:198
  107.7 0.9 copy-done.1
  108.6 10.4 %all-to-all-start.1 = ((bf16[64,2,2304]{2,1,0:T(2,128)(2,1)}), bf16[64,2,2304]{2,1,0:T(2,128)(2,1)S(1)}, u32[]{:S(2)}, u32[]{:S(2)}) async-start(bf16[64,2,2304]{2,1,0:T(2,128)(2,1)} %reshape.235), calls=%async_computation.1 | async-start | bytes 1179648 | tf_op jit(solution)/shard_map/all_to_all | solution.py:97
  119.5 0.6 reduce.1
  120.0 1.2 reduce
  121.5 3.2 %fusion.12 = f32[512,512]{1,0:T(8,128)} fusion(bf16[1,896,512]{2,1,0:T(8,128)(2,1)} %param.26, bf16[64,8,896]{2,1,0:T(8,128)(2,1)} %copy-done.1), kind=kOutput, calls=%fused_computation.27 | convolution fusion | flops 469762048 | bytes 2883584 | tf_op jit(solution)/shard_map/dot_general | solution.py:202
  124.7 1.7 fusion.14
  126.7 23.0 %all-to-all-done.1 = bf16[64,2,2304]{2,1,0:T(2,128)(2,1)S(1)} async-done(((bf16[64,2,2304]{2,1,0:T(2,128)(2,1)}), bf16[64,2,2304]{2,1,0:T(2,128)(2,1)S(1)}, u32[]{:S(2)}, u32[]{:S(2)}) %all-to-all-start.1) | async-done | bytes 589856 | tf_op jit(solution)/shard_map/all_to_all | solution.py:97
  149.6 0.5 reshape.236
  150.1 0.2 convolution_convert_fusion.1
  150.4 0.3 reshape.193
  150.9 1.5 fusion.60
  152.4 1.5 fusion.23
  153.9 56.3 %all-reduce.3.cloned.1.call-done = (f32[512,512]{1,0:T(8,128)}, f32[512,512]{1,0:T(8,128)}) async-done(((f32[512,512]{1,0:T(8,128)}, f32[512,512]{1,0:T(8,128)}), (f32[512,512]{1,0:T(8,128)}, f32[512,512]{1,0:T(8,128)})) %all-reduce.3.cloned.1.call-update) | async-done | bytes 2097168 | tf_op jit(solution)/shard_map/psum | solution.py:203
  210.2 3.2 %fusion.5 = bf16[64,8,896]{2,1,0:T(8,128)(2,1)} fusion(bf16[1,512,896]{2,1,0:T(8,128)(2,1)S(1)} %copy-done, f32[512,512]{1,0:T(8,128)} %get-tuple-element.56, f32[512,512]{1,0:T(8,128)} %get-tuple-element.57), kind=kOutput, calls=%fused_computation.14 | convolution fusion | flops 471793664 | bytes 3932160 | tf_op jit(solution)/shard_map/dot_general | solution.py:205
  213.4 15.3 %all-to-all-start.4 = ((bf16[64,8,896]{2,1,0:T(8,128)(2,1)}), bf16[64,8,896]{2,1,0:T(8,128)(2,1)S(1)}, u32[]{:S(2)}, u32[]{:S(2)}) async-start(bf16[64,8,896]{2,1,0:T(8,128)(2,1)} %fusion.5), calls=%async_computation.4 | async-start | bytes 1835008 | tf_op jit(solution)/shard_map/all_to_all | solution.py:207
  228.9 0.3 convolution_convert_fusion.6
  229.3 10.1 %all-gather.3 = f32[8,4,128]{2,1,0:T(4,128)S(1)} all-gather(f32[1,4,128]{2,1,0:T(4,128)S(1)} %bitcast.86), channel_id=2, replica_groups=mesh['tp'=8,'dp'=64] {'tp'}, dimensions={0}, use_global_device_ids=true | all-gather | bytes 18432 | tf_op jit(solution)/shard_map/all_gather | solution.py:14
  239.6 11.3 %all-gather.4 = f32[8,4,128]{2,1,0:T(4,128)S(1)} all-gather(f32[1,4,128]{2,1,0:T(4,128)S(1)} %bitcast.87), channel_id=3, replica_groups=mesh['tp'=8,'dp'=64] {'tp'}, dimensions={0}, use_global_device_ids=true | all-gather | bytes 18432 | tf_op jit(solution)/shard_map/all_gather | solution.py:14
  250.9 27.6 %all-to-all-done.4 = bf16[64,8,896]{2,1,0:T(8,128)(2,1)S(1)} async-done(((bf16[64,8,896]{2,1,0:T(8,128)(2,1)}), bf16[64,8,896]{2,1,0:T(8,128)(2,1)S(1)}, u32[]{:S(2)}, u32[]{:S(2)}) %all-to-all-start.4) | async-done | bytes 917536 | tf_op jit(solution)/shard_map/all_to_all | solution.py:207
  278.5 0.9 convolution_convert_fusion.4
  279.4 7.6 %slice.43 = f32[28,128,512]{2,1,0:T(8,128)} slice(f32[32,128,512]{2,1,0:T(8,128)} %all-gather.7.cloned.1.call-done), slice={[4:32], [0:128], [0:512]} | slice | bytes 14680064 | tf_op jit(solution)/shard_map/slice | solution.py:16
  287.0 11.0 %while.14 = (s32[]{:T(128)}, f32[4,128]{1,0:T(4,128)S(1)}, f32[4,128]{1,0:T(4,128)S(1)}, f32[4,128,512]{2,1,0:T(8,128)S(1)}, f32[7,4,128]{2,1,0:T(4,128)S(1)}, /...) while((s32[]{:T(128)}, f32[4,128]{1,0:T(4,128)S(1)}, f32[4,128]{1,0:T(4,128)S(1)}, ...), condition=%wide.region_6.7_spmd, body=%wide.region_5.6_spmd.sunk | while | flops 789506 | bytes 3166309 | solution.py:17
  287.0 1.5 fusion.68
  288.6 1.5 fusion.68
  290.2 1.5 fusion.68
  291.7 1.5 fusion.68
  293.3 1.5 fusion.68
  294.9 1.5 fusion.68
  296.4 1.5 fusion.68
  298.0 0.7 divide_convert_fusion
  (64 shorter events, 2.9 us)
Async XLA Ops:
  7.2 203.0 %copy-start = (bf16[1,512,896]{2,1,0:T(8,128)(2,1)S(1)}, bf16[1,512,896]{2,1,0:T(8,128)(2,1)}, u32[]{:S(2)}) copy-start(bf16[1,512,896]{2,1,0:T(8,128)(2,1)} %param.27) | copy-start | bytes 2752516
  9.8 32.1 %all-to-all-start.2 = ((bf16[64,1,1]{2,1,0:T(2,128)(2,1)}), bf16[64,1,1]{2,1,0:T(2,128)(2,1)S(1)}, u32[]{:S(2)}, u32[]{:S(2)}) async-start(bf16[64,1,1]{2,1,0:T(2,128)(2,1)} %copy.55), calls=%async_computation.2 | async-start | bytes 65536 | tf_op jit(solution)/shard_map/all_to_all | solution.py:111
  30.0 34.6 %copy-start.3 = (bf16[32,8,576]{2,1,0:T(8,128)(2,1)S(1)}, bf16[32,8,576]{2,1,0:T(8,128)(2,1)}, u32[]{:S(2)}) copy-start(bf16[32,8,576]{2,1,0:T(8,128)(2,1)} %param.19) | copy-start | bytes 884740
  41.9 18.1 %all-to-all-start = ((s32[64,1,1]{2,1,0:T(1,128)}), s32[64,1,1]{2,1,0:T(1,128)S(1)}, u32[]{:S(2)}, u32[]{:S(2)}) async-start(s32[64,1,1]{2,1,0:T(1,128)} %copy.51), calls=%async_computation | async-start | bytes 65536 | tf_op jit(solution)/shard_map/all_to_all | solution.py:104
  60.0 47.7 %all-to-all-start.3 = ((bf16[64,8,896]{2,1,0:T(8,128)(2,1)}), bf16[64,8,896]{2,1,0:T(8,128)(2,1)S(1)}, u32[]{:S(2)}, u32[]{:S(2)}) async-start(bf16[64,8,896]{2,1,0:T(8,128)(2,1)} %fusion.4), calls=%async_computation.3 | async-start | bytes 1835008 | tf_op jit(solution)/shard_map/all_to_all | solution.py:198
  65.3 53.7 %copy-start.7 = (bf16[32]{0:T(256)(128)(2,1)S(1)}, bf16[32]{0:T(256)(128)(2,1)}, u32[]{:S(2)}) copy-start(bf16[32]{0:T(256)(128)(2,1)} %param.18) | copy-start | bytes 196
  65.3 53.8 %copy-start.4 = (bf16[32,8,576]{2,1,0:T(8,128)(2,1)S(1)}, bf16[32,8,576]{2,1,0:T(8,128)(2,1)}, u32[]{:S(2)}) copy-start(bf16[32,8,576]{2,1,0:T(8,128)(2,1)} %param.17) | copy-start | bytes 884740
  65.9 53.5 %copy-start.8 = (s32[4]{0:T(128)S(1)}, s32[4]{0:T(128)}, u32[]{:S(2)}) copy-start(s32[4]{0:T(128)} %param.16) | copy-start | bytes 52
  107.7 0.9 copy-start.1
  108.6 41.0 %all-to-all-start.1 = ((bf16[64,2,2304]{2,1,0:T(2,128)(2,1)}), bf16[64,2,2304]{2,1,0:T(2,128)(2,1)S(1)}, u32[]{:S(2)}, u32[]{:S(2)}) async-start(bf16[64,2,2304]{2,1,0:T(2,128)(2,1)} %reshape.235), calls=%async_computation.1 | async-start | bytes 1179648 | tf_op jit(solution)/shard_map/all_to_all | solution.py:97
  119.0 91.2 %all-reduce.3.cloned.1.call-start = ((), (), s32[]{:S(2)}) async-start(), calls=%async_computation.6 | async-start | bytes 4194304 | tf_op jit(solution)/shard_map/psum | solution.py:203
  119.2 5.5 %copy-start.2 = (bf16[64,8,896]{2,1,0:T(8,128)(2,1)S(1)}, bf16[64,8,896]{2,1,0:T(8,128)(2,1)}, u32[]{:S(2)}) copy-start(bf16[64,8,896]{2,1,0:T(8,128)(2,1)} %copy-done.1) | copy-start | bytes 2752516
  121.3 3.4 %copy-start.6 = (bf16[1,896,512]{2,1,0:T(8,128)(2,1)S(1)}, bf16[1,896,512]{2,1,0:T(8,128)(2,1)}, u32[]{:S(2)}) copy-start(bf16[1,896,512]{2,1,0:T(8,128)(2,1)} %param.25) | copy-start | bytes 2752516
  126.5 153.0 %all-gather.7.cloned.1.call-start = ((), (), s32[]{:S(2)}) async-start(), calls=%async_computation.5 | async-start | bytes 9437184 | tf_op jit(solution)/shard_map/all_gather | solution.py:14
  213.4 15.4 %copy-start.5 = (bf16[16,8]{0,1:T(8,128)(2,1)S(1)}, bf16[16,8]{0,1:T(8,128)(2,1)}, u32[]{:S(2)}) copy-start(bf16[16,8]{0,1:T(8,128)(2,1)} %param.24) | copy-start | bytes 772
  213.4 65.1 %all-to-all-start.4 = ((bf16[64,8,896]{2,1,0:T(8,128)(2,1)}), bf16[64,8,896]{2,1,0:T(8,128)(2,1)S(1)}, u32[]{:S(2)}, u32[]{:S(2)}) async-start(bf16[64,8,896]{2,1,0:T(8,128)(2,1)} %fusion.5), calls=%async_computation.4 | async-start | bytes 1835008 | tf_op jit(solution)/shard_map/all_to_all | solution.py:207
  279.4 7.6 %slice-start = ((f32[32,128,512]{2,1,0:T(8,128)}), f32[4,128,512]{2,1,0:T(8,128)S(1)}, s32[]{:S(2)}) async-start(f32[32,128,512]{2,1,0:T(8,128)} %all-gather.7.cloned.1.call-done), calls=%async_computation.7 | async-start | bytes 2097152 | tf_op jit(solution)/shard_map/slice | solution.py:15
Sparse Core Ops, SparseCore 0:
  126.6 83.5 all-reduce.2
  212.3 56.5 all-gather.6
where the time goes:
time: 307 us; the launch traced here: 306 us
  waiting for transfers between devices  169 us (55%)
  starting transfers between devices  53.5 us (17%)
  blocking collectives  21.4 us (7%)
  matrix products  16.3 us (5%)
  other arithmetic  16.2 us (5%)
  local copies, waits for them, and re-layouts  14.5 us (5%)
  between operations  14.3 us (5%)
    psum x1, waiting for transfers between devices, on_device(): gate_sum, up_sum = lax.psum((gate_part, up_part), 'tp')  56.3 us
    all_to_all x1, waiting for transfers between devices, on_device(): lax.all_to_all(outgoing, 'dp', split_axis=0, concat_axis=0, tiled=True)  39.8 us
    all_to_all x1, waiting for transfers between devices, on_device(): lax.all_to_all(outputs, 'dp', split_axis=0, concat_axis=0, tiled=True)  27.6 us
    all_to_all x1, waiting for transfers between devices, on_device(): lax.all_to_all(sent_pages.reshape(n_dp, page_capacity, per_page * key_val...  23 us
    all_gather x2, blocking collectives, combined_all(): pieces = jax.tree.map(lambda part: lax.all_gather(part, axis), value)  21.4 us
    all_to_all x1, starting transfers between devices, on_device(): lax.all_to_all(sent_scales.reshape(n_dp, page_capacity), 'dp', split_axis...  18.4 us
    all_to_all x1, starting transfers between devices, on_device(): lax.all_to_all(outputs, 'dp', split_axis=0, concat_axis=0, tiled=True)  15.3 us
    all_to_all x1, waiting for transfers between devices, on_device(): lax.all_to_all(sent_position.reshape(n_dp, page_capacity), 'dp', split_ax...  11.4 us
  transfers between devices with their start and end apart: 7, of which 6 were waited for; matrix products, arithmetic and copies ran while one was open for 8% of the time, Pallas kernels for 0%

commit v1 on v0

v1 whole, which is shorter than its diff:
```python
import jax
import jax.numpy as jnp
from jax import lax
from jax.experimental import pallas as pl
from jax.experimental.pallas import tpu as pltpu
from jax.sharding import PartitionSpec as P

F32, BF16, I32 = jnp.float32, jnp.bfloat16, jnp.int32
MESH = pl.DeviceIdType.MESH
FACTOR = 192.0 ** (-0.5)
MASKED = -1e30
NZ, NY, NX = 16, 4, 4
QN = 4
WD = 896
ORDER = [0, 15, 1, 14, 2, 13, 3, 12, 4, 11, 5, 10, 6, 9, 7, 8]
PLACE = {rel: k for k, rel in enumerate(ORDER)}


def dot(a, b, ca=1, cb=0):
    return lax.dot_general(a, b, (((ca,), (cb,)), ((), ())), preferred_element_type=F32)


def iota(shape, dim):
    return lax.broadcasted_iota(I32, shape, dim)


def kernel(
    queries, lengths, resident, resident_scale, pages, prefill_scale, page_slot,
    tokens, ids, gates, gate_w, up_w, down_w,
    att_out, moe_out,
    v_gate, v_up, v_down, zbuf, dsend, ffn_x, gu, core_send, core_recv, x_send, x_recv,
    h_all, r_buf, p_buf, zs, zr, own_sum,
    page_tail, pg_send, pg_recv, pg_turn, pg_slots, new_k, scores, ml_all, at_send, at_recv,
    load_sem, tok_sem, ring_s, ring_r, yd_s, yd_r, co_s, co_r, xx_s, xx_r, hh_s, hh_r,
    yr_s, yr_r, zr_s, zr_r, pz_s, pz_r, py_s, py_r, ml_s, ml_r, at_s, at_r,
):
    tp = lax.axis_index("tp")
    dp = lax.axis_index("dp")
    x, c = tp // 2, tp % 2
    z, y = dp // NY, dp % NY

    def at_dp(zz, yy):
        return {"dp": zz * NY + yy}

    def z_peer(d):
        return at_dp(lax.rem(z + d, NZ), y)

    def y_peer(d):
        return lax.rem(y + d, NY)

    def tp_peer(d):
        return lax.rem(tp + d, 8)

    def x_peer(d):
        return lax.rem(x + d, NX)

    sibling = x * 2 + (1 - c)

    def rows(ref, start, size):
        if not isinstance(start, int):
            start = pl.multiple_of(start, 8 if size % 16 else 16)
        return ref.at[pl.ds(start, size), :]

    started = []

    def remote(src, dst, ssem, rsem, where):
        return pltpu.make_async_remote_copy(
            src_ref=src, dst_ref=dst, send_sem=ssem, recv_sem=rsem,
            device_id=where, device_id_type=MESH,
        )

    def send(src, dst, ssem, rsem, where):
        copy = remote(src, dst, ssem, rsem, where)
        copy.start()
        started.append(copy)

    def arrive(dst, rsem, ssem, where):
        remote(dst, dst, ssem, rsem, where).wait_recv()

    tok_copy = pltpu.make_async_copy(
        tokens.at[:, pl.ds(pl.multiple_of(tp * WD, 128), WD)], zbuf.at[pl.ds(0, 16), pl.ds(0, WD)], tok_sem
    )
    tok_copy.start()
    loads = [
        pltpu.make_async_copy(gate_w, v_gate, load_sem.at[0]),
        pltpu.make_async_copy(up_w, v_up, load_sem.at[1]),
        pltpu.make_async_copy(down_w, v_down, load_sem.at[2]),
    ]
    for copy in loads:
        copy.start()

    barrier = pltpu.get_barrier_semaphore()
    for d in range(1, NZ):
        pl.semaphore_signal(barrier, inc=1, device_id=z_peer(d), device_id_type=MESH)
    for d in range(1, NY):
        pl.semaphore_signal(barrier, inc=1, device_id=at_dp(z, y_peer(d)), device_id_type=MESH)
    for d in range(1, 8):
        pl.semaphore_signal(barrier, inc=1, device_id={"tp": tp_peer(d)}, device_id_type=MESH)

    lane = iota((16, 128), 1)
    idv = ids[...]
    gwv = gates[...].astype(F32)
    chosen = jnp.zeros((16, 128), F32)
    gate_l = jnp.zeros((16, 128), F32)
    for k in range(8):
        chosen += jnp.where(idv[:, k : k + 1] == lane, 1.0, 0.0)
        gate_l += jnp.where(idv[:, k : k + 1] + 32 == lane, gwv[:, k : k + 1], 0.0)
    before = (iota((16, 16), 1) < iota((16, 16), 0)).astype(BF16)
    rank = dot(before, chosen.astype(BF16))
    zbuf[0:16, WD:1024] = (chosen * (rank + 1.0) + gate_l).astype(BF16)
    tok_copy.wait()
    pl.semaphore_wait(barrier, NZ - 1 + NY - 1 + 7)

    def ring(s):
        right = (NZ - s) % NZ
        send(
            rows(zbuf, 16 * PLACE[right], 16), rows(zbuf, 16 * PLACE[right - 1 if right else 15], 16),
            ring_s.at[right - 1 if right else 15], ring_r.at[right - 1 if right else 15], z_peer(1),
        )
        if s < 7:
            send(
                rows(zbuf, 16 * PLACE[s], 16), rows(zbuf, 16 * PLACE[s + 1], 16),
                ring_s.at[s + 1], ring_r.at[s + 1], z_peer(NZ - 1),
            )

    def ring_wait(s):
        got = NZ - 1 - s
        arrive(rows(zbuf, 16 * PLACE[got], 16), ring_r.at[got], ring_s.at[got], z_peer(1))
        if s < 7:
            arrive(rows(zbuf, 16 * PLACE[s + 1], 16), ring_r.at[s + 1], ring_s.at[s + 1], z_peer(NZ - 1))

    e0 = 2 * z

    def dispatch(q):
        meta = zbuf[64 * q : 64 * q + 64, WD:1024]
        pick = (iota((16, 128), 1) == e0 + iota((16, 128), 0)).astype(BF16)
        slots = dot(pick, meta, 1, 1).astype(I32)
        col = iota((1, 64), 1)
        base = col // 16 * 8 - 1
        t0 = jnp.where(slots[0:1] > 0, slots[0:1] + base, -1)
        t1 = jnp.where(slots[1:2] > 0, slots[1:2] + base + 32, -1)
        row = iota((64, 64), 0)
        g = jnp.where(row == jnp.where(row < 32, t0, t1), 1.0, 0.0).astype(BF16)
        dsend[64 * q : 64 * q + 64, :] = dot(g, zbuf[64 * q : 64 * q + 64, 0:WD]).astype(BF16)
        for d in range(1, NY):
            to = y_peer(d)
            send(
                rows(dsend, 64 * q + to // 2 * 32, 32), rows(ffn_x, 128 * q + y * 32, 32),
                yd_s.at[q, d], yd_r.at[q, d], at_dp(z, to),
            )
        own = dsend[pl.ds(pl.multiple_of(64 * q + y // 2 * 32, 32), 32), :]
        ffn_x[pl.ds(pl.multiple_of(128 * q + y * 32, 32), 32), :] = own

    def first_ffn(q):
        if q == 0:
            loads[0].wait()
            loads[1].wait()
        for d in range(1, NY):
            arrive(rows(ffn_x, 128 * q + y_peer(NY - d) * 32, 32), yd_r.at[q, d], yd_s.at[q, d], at_dp(z, y_peer(d)))
        a = ffn_x[128 * q : 128 * q + 128, :]
        gu[128 * q : 128 * q + 128, 0:512] = dot(a, v_gate[...])
        gu[128 * q : 128 * q + 128, 512:1024] = dot(a, v_up[...])
        theirs = gu[pl.ds(pl.multiple_of(128 * q + (1 - c) * 64, 64), 64), :]
        core_send[64 * q : 64 * q + 64, :] = theirs.astype(BF16)
        send(
            rows(core_send, 64 * q, 64), rows(core_recv, 64 * q, 64), co_s.at[q], co_r.at[q], {"tp": sibling}
        )

    def over_x(q):
        arrive(rows(core_recv, 64 * q, 64), co_r.at[q], co_s.at[q], {"tp": sibling})
        mine = gu[pl.ds(pl.multiple_of(128 * q + c * 64, 64), 64), :]
        own_sum[64 * q : 64 * q + 64, :] = mine + core_recv[64 * q : 64 * q + 64, :].astype(F32)
        x_send[64 * q : 64 * q + 64, :] = own_sum[64 * q : 64 * q + 64, :].astype(BF16)
        for d in range(1, NX):
            to = x_peer(d)
            send(
                rows(x_send, 64 * q + to * 16, 16), rows(x_recv, 64 * q + x * 16, 16),
                xx_s.at[q, d], xx_r.at[q, d], {"tp": to * 2 + c},
            )

    def hidden(q):
        for d in range(1, NX):
            arrive(rows(x_recv, 64 * q + x_peer(NX - d) * 16, 16), xx_r.at[q, d], xx_s.at[q, d], {"tp": x_peer(d) * 2 + c})
        total = own_sum[pl.ds(pl.multiple_of(64 * q + x * 16, 16), 16), :]
        for d in range(1, NX):
            total += x_recv[pl.ds(pl.multiple_of(64 * q + x_peer(d) * 16, 16), 16), :].astype(F32)
        gv, uv = total[:, 0:512], total[:, 512:1024]
        hid = gv / (1.0 + jnp.exp(-gv)) * uv
        place = 128 * q + c * 64 + x * 16
        h_all[pl.ds(pl.multiple_of(place, 16), 16), :] = hid.astype(BF16)
        for d in range(1, 8):
            send(
                rows(h_all, place, 16), rows(h_all, place, 16), hh_s.at[q, d], hh_r.at[q, d], {"tp": tp_peer(d)}
            )

    def second_ffn(q):
        if q == 0:
            loads[2].wait()
        for d in range(1, 8):
            src = tp_peer(8 - d)
            arrive(
                rows(h_all, 128 * q + src % 2 * 64 + src // 2 * 16, 16),
                hh_r.at[q, d], hh_s.at[q, d], {"tp": tp_peer(d)},
            )
        r_buf[128 * q : 128 * q + 128, :] = dot(h_all[128 * q : 128 * q + 128, :], v_down[...]).astype(BF16)
        for d in range(1, NY):
            to = y_peer(d)
            send(
                rows(r_buf, 128 * q + to * 32, 32), rows(p_buf, 128 * q + y * 32, 32),
                yr_s.at[q, d], yr_r.at[q, d], at_dp(z, to),
            )
        place = pl.ds(pl.multiple_of(128 * q + y * 32, 32), 32)
        p_buf[place, :] = r_buf[place, :]

    def combine(q):
        for d in range(1, NY):
            arrive(rows(p_buf, 128 * q + y_peer(NY - d) * 32, 32), yr_r.at[q, d], yr_s.at[q, d], at_dp(z, y_peer(d)))
        meta = zbuf[64 * q : 64 * q + 64, WD:1024].astype(F32)
        ln = iota((64, 128), 1)

        def column(at):
            return jnp.sum(jnp.where(ln == at, meta, 0.0), axis=1, keepdims=True)

        base = iota((64, 1), 0) // 16 * 8 - 1
        col = iota((64, 128), 1)
        s0, s1 = column(e0).astype(I32), column(e0 + 1).astype(I32)
        t0 = jnp.where(s0 > 0, s0 + base, -1)
        t1 = jnp.where(s1 > 0, s1 + base, -1)
        g0, g1 = column(e0 + 32), column(e0 + 33)
        target = jnp.where(col < 64, t0, t1)
        gate = jnp.where(col < 64, g0, g1)
        mix = jnp.where(col % 32 == target, gate, 0.0).astype(BF16)
        zs[64 * q : 64 * q + 64, :] = dot(mix, p_buf[128 * q : 128 * q + 128, :]).astype(BF16)
        for k in range(4 * q, 4 * q + 4):
            rel = ORDER[k]
            if rel:
                back = PLACE[NZ - rel]
                send(rows(zs, 16 * k, 16), rows(zr, 16 * back, 16), zr_s.at[back], zr_r.at[back], z_peer(rel))

    def finish_moe():
        total = zs[0:16, :].astype(F32)
        for k in range(1, NZ):
            arrive(rows(zr, 16 * k, 16), zr_r.at[k], zr_s.at[k], z_peer(1))
            total += zr[16 * k : 16 * k + 16, :].astype(F32)
        moe_out[...] = total.astype(BF16)

    def expand(vector):
        spread = (iota((256, 32), 0) // 8 == iota((256, 32), 1)).astype(BF16)
        return dot(spread, vector, 1, 1)

    def pack_pages():
        slot = page_slot[...]
        target, position = slot // 32, slot % 32
        r16 = iota((64, 32), 0)
        sel = jnp.where(r16 == 0, (position + 1).astype(F32), jnp.where(r16 == 1, prefill_scale[...].astype(F32), 0.0))
        page_tail[:, 0:64] = pages[:, 512:576]
        page_tail[:, 64:128] = expand(sel.astype(BF16)).astype(BF16)
        spread = (iota((32, 256), 1) // 8 == iota((32, 256), 0)).astype(BF16)
        wide = jnp.broadcast_to(target.astype(F32), (16, 32)).astype(BF16)
        goal = dot(wide, spread)[0:1].astype(I32) * 8 + iota((1, 256), 1) % 8
        put = jnp.where(iota((512, 256), 0) == goal, 1.0, 0.0).astype(BF16)
        pg_send[:, 0:512] = dot(put, pages[:, 0:512]).astype(BF16)
        pg_send[:, 512:640] = dot(put, page_tail[...]).astype(BF16)

    def send_pages():
        for d in range(1, NZ):
            to = lax.rem(z + d, NZ)
            send(rows(pg_send, to * 32, 32), rows(pg_recv, z * 32, 32), pz_s.at[d], pz_r.at[d], z_peer(d))
        place = pl.ds(pl.multiple_of(z * 32, 32), 32)
        pg_recv[place, :] = pg_send[place, :]

    def turn_pages():
        for d in range(1, NZ):
            arrive(rows(pg_recv, lax.rem(z + NZ - d, NZ) * 32, 32), pz_r.at[d], pz_s.at[d], z_peer(d))
        r = iota((512, 512), 0)
        src = r % 128 // 8 * 32 + r // 128 * 8 + r % 8
        turn = jnp.where(iota((512, 512), 1) == src, 1.0, 0.0).astype(BF16)
        pg_turn[...] = dot(turn, pg_recv[...]).astype(BF16)
        for d in range(1, NY):
            to = y_peer(d)
            send(rows(pg_turn, to * 128, 128), rows(pg_slots, y * 128, 128), py_s.at[d], py_r.at[d], at_dp(z, to))
        place = pl.ds(pl.multiple_of(y * 128, 128), 128)
        pg_slots[place, :] = pg_turn[place, :]

    def place_pages():
        for d in range(1, NY):
            arrive(rows(pg_slots, y_peer(NY - d) * 128, 128), py_r.at[d], py_s.at[d], at_dp(z, y_peer(d)))
        pick = (iota((16, 128), 1) == 64).astype(BF16)
        position = dot(pick, pg_slots[:, 512:640], 1, 1)[0:1].astype(I32)
        goal = jnp.where(position > 0, (position - 1) * 8 + iota((1, 512), 1) % 8, -1)
        take = jnp.where(iota((256, 512), 0) == goal, 1.0, 0.0).astype(BF16)
        new_k[...] = dot(take, pg_slots[...]).astype(BF16)

    def score(r):
        if r < 2:
            k0 = resident[128 * r : 128 * r + 128, 0:512]
            k1 = resident[128 * r : 128 * r + 128, 512:576]
            wide = jnp.broadcast_to(resident_scale[...].astype(F32), (16, 32)).astype(BF16)
            spread = (iota((128, 32), 0) // 8 + 16 * r == iota((128, 32), 1)).astype(BF16)
            scale = dot(spread, wide, 1, 1)[:, 0:1]
        else:
            k0 = new_k[128 * r - 256 : 128 * r - 128, 0:512]
            k1 = new_k[128 * r - 256 : 128 * r - 128, 512:576]
            scale = new_k[128 * r - 256 : 128 * r - 128, 512:640].astype(F32)[:, 65:66]
        s = dot(k0, queries[r, :, 0:512], 1, 1) + dot(k1, queries[r, :, 512:576], 1, 1)
        local = iota((128, 128), 0)
        seen = local // 8 * 64 + tp * 8 + local % 8 < lengths[r]
        s = jnp.where(seen, s * (scale * FACTOR), MASKED)
        scores[128 * r : 128 * r + 128, :] = s
        m = jnp.max(s, axis=0, keepdims=True)
        l = jnp.sum(jnp.where(seen, jnp.exp(s - m), 0.0), axis=0, keepdims=True)
        ml_all[pl.ds(pl.multiple_of(tp * 8, 8), 8), :] = jnp.where(
            iota((8, 128), 0) == r, m,
            jnp.where(iota((8, 128), 0) == r + 4, l, ml_all[pl.ds(pl.multiple_of(tp * 8, 8), 8), :]),
        )

    def clear_ml():
        ml_all[pl.ds(pl.multiple_of(tp * 8, 8), 8), :] = jnp.zeros((8, 128), F32)

    def send_ml():
        place = rows(ml_all, tp * 8, 8)
        for d in range(1, 8):
            send(place, place, ml_s.at[d], ml_r.at[d], {"tp": tp_peer(d)})

    def weigh():
        for d in range(1, 8):
            arrive(rows(ml_all, tp_peer(8 - d) * 8, 8), ml_r.at[d], ml_s.at[d], {"tp": tp_peer(d)})
        highest = ml_all[0:4, :]
        for i in range(1, 8):
            highest = jnp.maximum(highest, ml_all[8 * i : 8 * i + 4, :])
        total = jnp.zeros((4, 128), F32)
        for i in range(8):
            total += ml_all[8 * i + 4 : 8 * i + 8, :] * jnp.exp(ml_all[8 * i : 8 * i + 4, :] - highest)
        inverse = 1.0 / total
        for r in range(4):
            s = scores[128 * r : 128 * r + 128, :]
            local = iota((128, 128), 0)
            seen = local // 8 * 64 + tp * 8 + local % 8 < lengths[r]
            if r < 2:
                value = resident[128 * r : 128 * r + 128, 0:512]
                wide = jnp.broadcast_to(resident_scale[...].astype(F32), (16, 32)).astype(BF16)
                spread = (iota((128, 32), 0) // 8 + 16 * r == iota((128, 32), 1)).astype(BF16)
                scale = dot(spread, wide, 1, 1)[:, 0:1]
            else:
                value = new_k[128 * r - 256 : 128 * r - 128, 0:512]
                scale = new_k[128 * r - 256 : 128 * r - 128, 512:640].astype(F32)[:, 65:66]
            w = jnp.where(seen, jnp.exp(s - highest[r : r + 1]), 0.0) * (scale * inverse[r : r + 1])
            part = dot(w.T.astype(BF16), value).astype(BF16)
            for i in range(8):
                at_send[64 * i + 16 * r : 64 * i + 16 * r + 16, :] = part[16 * i : 16 * i + 16, :]
        for d in range(1, 8):
            to = tp_peer(d)
            send(rows(at_send, to * 64, 64), rows(at_recv, tp * 64, 64), at_s.at[d], at_r.at[d], {"tp": to})

    def finish_attention():
        total = at_send[pl.ds(pl.multiple_of(tp * 64, 64), 64), :].astype(F32)
        for d in range(1, 8):
            src = tp_peer(8 - d)
            arrive(rows(at_recv, src * 64, 64), at_r.at[d], at_s.at[d], {"tp": tp_peer(d)})
            total += at_recv[pl.ds(pl.multiple_of(src * 64, 64), 64), :].astype(F32)
        total = total.astype(BF16)
        for r in range(4):
            att_out[r] = total[16 * r : 16 * r + 16, :]

    def both(s):
        ring(s)
        ring_wait(s)

    ring(0)
    pack_pages()
    ring_wait(0)
    both(1)
    dispatch(0)
    both(2)
    both(3)
    dispatch(1)
    both(4)
    both(5)
    dispatch(2)
    both(6)
    ring(7)
    first_ffn(0)
    ring_wait(7)
    dispatch(3)
    send_pages()
    first_ffn(1)
    over_x(0)
    first_ffn(2)
    over_x(1)
    hidden(0)
    first_ffn(3)
    over_x(2)
    hidden(1)
    second_ffn(0)
    over_x(3)
    hidden(2)
    second_ffn(1)
    combine(0)
    hidden(3)
    clear_ml()
    score(0)
    score(1)
    second_ffn(2)
    combine(1)
    second_ffn(3)
    combine(2)
    turn_pages()
    combine(3)
    place_pages()
    score(2)
    score(3)
    send_ml()
    weigh()
    finish_moe()
    finish_attention()
    for copy in started:
        copy.wait_send()


def on_device(
    queries, lengths, resident_pages, resident_scale, prefill_written_pages, prefill_scale,
    page_slot, tokens, expert_ids, gate_weights, gate_projection, up_weights, down_weights,
):
    vmem = pl.BlockSpec(memory_space=pltpu.VMEM)
    smem = pl.BlockSpec(memory_space=pltpu.SMEM)
    hbm = pl.BlockSpec(memory_space=pl.ANY)
    dma = pltpu.SemaphoreType.DMA
    return pl.pallas_call(
        kernel,
        out_shape=(
            jax.ShapeDtypeStruct((4, 16, 512), BF16),
            jax.ShapeDtypeStruct((16, WD), BF16),
        ),
        in_specs=[vmem, smem, vmem, vmem, vmem, vmem, vmem, hbm, vmem, vmem, hbm, hbm, hbm],
        out_specs=(vmem, vmem),
        scratch_shapes=[
            pltpu.VMEM((WD, 512), BF16),
            pltpu.VMEM((WD, 512), BF16),
            pltpu.VMEM((512, WD), BF16),
            pltpu.VMEM((256, 1024), BF16),
            pltpu.VMEM((256, WD), BF16),
            pltpu.VMEM((512, WD), BF16),
            pltpu.VMEM((512, 1024), F32),
            pltpu.VMEM((256, 1024), BF16),
            pltpu.VMEM((256, 1024), BF16),
            pltpu.VMEM((256, 1024), BF16),
            pltpu.VMEM((256, 1024), BF16),
            pltpu.VMEM((512, 512), BF16),
            pltpu.VMEM((512, WD), BF16),
            pltpu.VMEM((512, WD), BF16),
            pltpu.VMEM((256, WD), BF16),
            pltpu.VMEM((256, WD), BF16),
            pltpu.VMEM((256, 1024), F32),
            pltpu.VMEM((256, 128), BF16),
            pltpu.VMEM((512, 640), BF16),
            pltpu.VMEM((512, 640), BF16),
            pltpu.VMEM((512, 640), BF16),
            pltpu.VMEM((512, 640), BF16),
            pltpu.VMEM((256, 640), BF16),
            pltpu.VMEM((512, 128), F32),
            pltpu.VMEM((64, 128), F32),
            pltpu.VMEM((512, 512), BF16),
            pltpu.VMEM((512, 512), BF16),
            dma((3,)),
            dma,
            dma((16,)), dma((16,)),
            dma((QN, 4)), dma((QN, 4)),
            dma((QN,)), dma((QN,)),
            dma((QN, 4)), dma((QN, 4)),
            dma((QN, 8)), dma((QN, 8)),
            dma((QN, 4)), dma((QN, 4)),
            dma((16,)), dma((16,)),
            dma((16,)), dma((16,)),
            dma((4,)), dma((4,)),
            dma((8,)), dma((8,)),
            dma((8,)), dma((8,)),
        ],
        compiler_params=pltpu.CompilerParams(
            collective_id=0, has_side_effects=True, vmem_limit_bytes=48 * 1024 * 1024
        ),
    )(
        queries,
        lengths,
        resident_pages.reshape(256, 576),
        resident_scale.reshape(1, 32),
        prefill_written_pages.reshape(256, 576),
        prefill_scale.reshape(1, 32),
        page_slot.reshape(1, 32),
        tokens,
        expert_ids,
        gate_weights,
        gate_projection.reshape(WD, 512),
        up_weights.reshape(WD, 512),
        down_weights.reshape(512, WD),
    )


def solution(mesh):
    placed = (
        P("dp", None, None), P("dp"), P("dp", "tp", None), P("dp"), P("dp", "tp", None), P("dp"),
        P("dp"), P("dp", None), P("dp", None), P("dp", None), P("dp", "tp", None),
        P("dp", "tp", None), P("dp", None, "tp"),
    )
    return jax.shard_map(
        on_device, mesh=mesh, in_specs=placed, out_specs=(P("dp", "tp", None), P("dp", "tp")),
        check_vma=False,
    )
```

time: 307 us -> 112 us (0.36)
  the two profiles are of different devices: /device:TPU:7 before, /device:TPU:1 now
where the time goes in v1:
time: 112 us; the launch traced here: 111 us
  Pallas kernels  102 us (91%)
  local copies, waits for them, and re-layouts  8.53 us (8%)
    pallas_call x1, Pallas kernels, on_device(): pl.pallas_call(kernel, out_shape=(jax.ShapeDtypeStruct((4, 16, 512), BF16...  102 us
    unnamed x25, local copies, waits for them, and re-layouts  8.53 us

profile of v1, /device:TPU:1, one launch (start us, length us, event | category | flops | bytes accessed | tf_op | source)
XLA Modules:
  0.0 110.8 jit_solution(3001865837029370644)
XLA Ops:
  0.6 0.0 copy-start
  0.6 0.8 copy.17.gates
  1.5 0.8 copy.16.ids
  2.2 0.0 copy-start.3
  2.2 0.0 copy-start.6
  2.2 0.0 copy-start.7
  2.2 0.0 copy-start.8
  2.3 0.0 copy-start.9
  2.3 1.4 %copy.15.queries = bf16[4,128,576]{2,1,0:T(8,128)(2,1)S(1)} copy(bf16[4,128,576]{1,2,0:T(8,128)(2,1)} %param.13) | data formatting | bytes 1179648 | tf_op args[0]
  3.7 0.0 copy-done
  3.7 0.0 copy-done.3
  3.7 0.0 copy-done.6
  3.7 0.0 copy-done.7
  3.7 0.0 copy-done.8
  3.7 0.0 copy-done.9
  3.7 0.0 copy-start.1
  3.7 1.2 %copy-done.1 = bf16[1,896,512]{2,1,0:T(8,128)(2,1)S(1)} copy-done((bf16[1,896,512]{2,1,0:T(8,128)(2,1)S(1)}, bf16[1,896,512]{2,1,0:T(8,128)(2,1)}, u32[]{:S(2)}) %copy-start.1) | copy-done | bytes 917528
  4.9 0.0 copy-start.2
  4.9 1.2 %copy-done.2 = bf16[1,512,896]{2,1,0:T(8,128)(2,1)S(1)} copy-done((bf16[1,512,896]{2,1,0:T(8,128)(2,1)S(1)}, bf16[1,512,896]{2,1,0:T(8,128)(2,1)}, u32[]{:S(2)}) %copy-start.2) | copy-done | bytes 917528
  6.1 0.0 copy-start.4
  6.1 1.0 copy-done.4
  7.1 0.0 copy-start.5
  7.1 0.9 copy-done.5
  8.0 101.6 %shard_map.140 = (bf16[4,16,512]{2,1,0:T(8,128)(2,1)S(1)}, bf16[16,896]{1,0:T(8,128)(2,1)S(1)}) custom-call(bf16[4,128,576]{2,1,0:T(8,128)(2,1)S(1)} %copy.15.queries, s32[4]{0:T(128)S(1)} %copy-done.6, bf16[256,576]{1,0:T(8,128)(2,1)S(1)} %bitcast.11, bf16[1,32]{1,0:T(2,128)(2,1)S(1)} %bitcast.13, bf16[256,576]{1,0:T(8,128)(2,1)S(1)} %bitcast.12, ...), custom_call_target="tpu_custom_call" | custom-call | tf_op jit(solution)/shard_map/pallas_call | solution.py:428
  109.6 0.6 copy.20
  110.2 0.6 copy.21
Async XLA Ops:
  0.6 3.0 %copy-start = (bf16[1,896,512]{2,1,0:T(8,128)(2,1)S(1)}, bf16[1,896,512]{2,1,0:T(8,128)(2,1)}, u32[]{:S(2)}) copy-start(bf16[1,896,512]{2,1,0:T(8,128)(2,1)} %param.23) | copy-start | bytes 2752516
  2.2 1.4 %copy-start.3 = (bf16[32,8,576]{2,1,0:T(8,128)(2,1)S(1)}, bf16[32,8,576]{2,1,0:T(8,128)(2,1)}, u32[]{:S(2)}) copy-start(bf16[32,8,576]{2,1,0:T(8,128)(2,1)} %param.15) | copy-start | bytes 884740
  2.2 1.4 %copy-start.6 = (s32[4]{0:T(128)S(1)}, s32[4]{0:T(128)}, u32[]{:S(2)}) copy-start(s32[4]{0:T(128)} %lengths.1) | copy-start | bytes 52
  2.2 1.5 %copy-start.7 = (bf16[32]{0:T(256)(128)(2,1)S(1)}, bf16[32]{0:T(256)(128)(2,1)}, u32[]{:S(2)}) copy-start(bf16[32]{0:T(256)(128)(2,1)} %param.16) | copy-start | bytes 196
  2.2 1.5 %copy-start.8 = (bf16[32]{0:T(256)(128)(2,1)S(1)}, bf16[32]{0:T(256)(128)(2,1)}, u32[]{:S(2)}) copy-start(bf16[32]{0:T(256)(128)(2,1)} %param.18) | copy-start | bytes 196
  2.3 1.5 %copy-start.9 = (s32[32]{0:T(128)S(1)}, s32[32]{0:T(128)}, u32[]{:S(2)}) copy-start(s32[32]{0:T(128)} %param.19) | copy-start | bytes 388
  3.7 1.2 %copy-start.1 = (bf16[1,896,512]{2,1,0:T(8,128)(2,1)S(1)}, bf16[1,896,512]{2,1,0:T(8,128)(2,1)}, u32[]{:S(2)}) copy-start(bf16[1,896,512]{2,1,0:T(8,128)(2,1)} %param.24) | copy-start | bytes 2752516
  4.9 1.2 %copy-start.2 = (bf16[1,512,896]{2,1,0:T(8,128)(2,1)S(1)}, bf16[1,512,896]{2,1,0:T(8,128)(2,1)}, u32[]{:S(2)}) copy-start(bf16[1,512,896]{2,1,0:T(8,128)(2,1)} %param.25) | copy-start | bytes 2752516
  6.1 1.0 copy-start.4
  7.1 0.9 copy-start.5

commit v2 on v1

v2 whole, which is shorter than its diff:
```python
import jax
import jax.numpy as jnp
from jax import lax
from jax.experimental import pallas as pl
from jax.experimental.pallas import tpu as pltpu
from jax.sharding import PartitionSpec as P

F32, BF16, I32 = jnp.float32, jnp.bfloat16, jnp.int32
MESH = pl.DeviceIdType.MESH
FACTOR = 192.0 ** (-0.5)
MASKED = -1e30
SCHEDULE = [
    "pack", "score 0", "score 1", "enter", "far", "send_att 0", "far_wait", "near", "dispatch 0",
    "near_wait 1", "dispatch 1", "first 0", "near_wait 2", "dispatch 2", "over_x 0", "near_wait 3", "dispatch 3",
    "send_pages 0", "send_pages 1", "send_pages 2", "send_pages 3", "first 1", "hidden 0", "over_x 1", "first 2",
    "second 0", "hidden 1", "over_x 2", "first 3", "second 1", "hidden 2", "over_x 3", "combine 0", "second 2",
    "hidden 3", "combine 1", "turn 0", "second 3", "combine 2", "turn 1", "combine 3", "turn 2", "finish_att 0",
    "turn 3", "place", "gather", "score 2", "score 3", "send_att 1", "finish_moe", "finish_att 1",
]
NZ, NY, NX = 16, 4, 4
QN = 4
WD = 896
ORDER = [12, 0, 4, 8, 13, 1, 5, 9, 11, 15, 3, 7, 10, 14, 2, 6]
PAGE_ORDER = [8, 9, 7, 10, 6, 11, 5, 12, 4, 13, 3, 14, 2, 15, 1, 0]


def dot(a, b, ca=1, cb=0):
    return lax.dot_general(a, b, (((ca,), (cb,)), ((), ())), preferred_element_type=F32)


def iota(shape, dim):
    return lax.broadcasted_iota(I32, shape, dim)


def kernel(
    queries, lengths, resident, resident_scale, pages, prefill_scale, page_slot,
    tokens, ids, gates, gate_w, up_w, down_w,
    att_out, moe_out,
    v_gate, v_up, v_down, v_q, v_res, v_pages, zbuf, dsend, ffn_x, gu, core_send, core_recv, x_send, x_recv,
    h_all, r_buf, p_buf, zs0, zs, ra, rb, rc, far_send, far_recv, own_sum,
    page_tail, pg_send, pg_recv, pg_turn, pg_slots, new_k, ml, at_send, at_recv, wcol,
    load_sem, zg_s, zg_r, yd_s, yd_r, co_s, co_r, xx_s, xx_r, hh_s, hh_r,
    yr_s, yr_r, rs_s, rs_r, pz_s, pz_r, py_s, py_r, ml_s, ml_r, at_s, at_r,
):
    tp = lax.axis_index("tp")
    dp = lax.axis_index("dp")
    x, c = tp // 2, tp % 2
    z, y = dp // NY, dp % NY

    def at_dp(zz, yy):
        return {"dp": zz * NY + yy}

    def z_peer(d):
        return at_dp(lax.rem(z + d, NZ), y)

    def y_peer(d):
        return lax.rem(y + d, NY)

    def tp_peer(d):
        return lax.rem(tp + d, 8)

    def x_peer(d):
        return lax.rem(x + d, NX)

    sibling = x * 2 + (1 - c)

    def span(start, size):
        if not isinstance(start, int):
            start = pl.multiple_of(start, 8 if size % 16 else 16)
        return pl.ds(start, size)

    def rows(ref, start, size):
        return ref.at[span(start, size), :]

    started = []

    def remote(src, dst, ssem, rsem, where):
        return pltpu.make_async_remote_copy(
            src_ref=src, dst_ref=dst, send_sem=ssem, recv_sem=rsem,
            device_id=where, device_id_type=MESH,
        )

    def send(src, dst, ssem, rsem, where):
        copy = remote(src, dst, ssem, rsem, where)
        copy.start()
        started.append(copy)

    def arrive(dst, rsem, ssem, where):
        remote(dst, dst, ssem, rsem, where).wait_recv()

    barrier = pltpu.get_barrier_semaphore()
    for d in range(1, NZ):
        pl.semaphore_signal(barrier, inc=1, device_id=z_peer(d), device_id_type=MESH)
    for d in range(1, NY):
        pl.semaphore_signal(barrier, inc=1, device_id=at_dp(z, y_peer(d)), device_id_type=MESH)
    for d in range(1, 8):
        pl.semaphore_signal(barrier, inc=1, device_id={"tp": tp_peer(d)}, device_id_type=MESH)

    local = [
        (tokens.at[:, pl.ds(pl.multiple_of(tp * WD, 128), WD)], zbuf.at[pl.ds(16, 16), pl.ds(0, WD)]),
        (pages, v_pages),
        (resident, v_res),
        (queries, v_q),
        (gate_w, v_gate),
        (up_w, v_up),
        (down_w, v_down),
    ]
    loads = [pltpu.make_async_copy(src, dst, load_sem.at[i]) for i, (src, dst) in enumerate(local)]
    for copy in loads:
        copy.start()

    lane = iota((16, 128), 1)
    idv = ids[...].astype(F32).T.astype(I32)
    gwv = gates[...].astype(F32).T
    chosen = jnp.zeros((16, 128), F32)
    gate_l = jnp.zeros((16, 128), F32)
    for k in range(8):
        chosen += jnp.where(idv[:, k : k + 1] == lane, 1.0, 0.0)
        gate_l += jnp.where(idv[:, k : k + 1] + 32 == lane, gwv[:, k : k + 1], 0.0)
    before = (iota((16, 16), 1) < iota((16, 16), 0)).astype(BF16)
    rank = dot(before, chosen.astype(BF16))
    zbuf[16:32, WD:1024] = (chosen * (rank + 1.0) + gate_l).astype(BF16)

    def enter():
        loads[0].wait()
        pl.semaphore_wait(barrier, NZ - 1 + NY - 1 + 7)

    def far():
        for i, d in enumerate((8, 4, 12)):
            send(rows(zbuf, 16, 16), rows(zbuf, 16 * ORDER.index(NZ - d), 16), zg_s.at[i], zg_r.at[i], z_peer(d))

    def far_wait():
        for i, d in enumerate((8, 4, 12)):
            arrive(rows(zbuf, 16 * ORDER.index(NZ - d), 16), zg_r.at[i], zg_s.at[i], z_peer(d))

    passing = [(NZ - 1, 0, 64, 64, 3), (1, 0, 128, 64, 4), (2, 0, 192, 32, 5), (NZ - 2, 16, 224, 32, 6)]

    def near():
        for d, at, there, size, i in passing:
            send(rows(zbuf, at, size), rows(zbuf, there, size), zg_s.at[i], zg_r.at[i], z_peer(d))

    def near_wait(q):
        for d, at, there, size, i in passing:
            if there // 64 == q:
                arrive(rows(zbuf, there, size), zg_r.at[i], zg_s.at[i], z_peer(d))

    e0 = 2 * z

    def dispatch(q):
        meta = zbuf[64 * q : 64 * q + 64, WD:1024]
        pick = (iota((16, 128), 1) == e0 + iota((16, 128), 0)).astype(BF16)
        slots = dot(pick, meta, 1, 1).astype(I32)
        base = iota((1, 64), 1) // 16 * 8 - 1
        t0 = jnp.where(slots[0:1] > 0, slots[0:1] + base, -1)
        t1 = jnp.where(slots[1:2] > 0, slots[1:2] + base + 32, -1)
        row = iota((64, 64), 0)
        g = jnp.where(row == jnp.where(row < 32, t0, t1), 1.0, 0.0).astype(BF16)
        dsend[64 * q : 64 * q + 64, :] = dot(g, zbuf[64 * q : 64 * q + 64, 0:WD]).astype(BF16)
        for d in (2, 1, 3):
            to = y_peer(d)
            send(
                rows(dsend, 64 * q + to // 2 * 32, 32), rows(ffn_x, 128 * q + y * 32, 32),
                yd_s.at[q, d], yd_r.at[q, d], at_dp(z, to),
            )
        ffn_x[span(128 * q + y * 32, 32), :] = dsend[span(64 * q + y // 2 * 32, 32), :]

    def first_ffn(q):
        if q == 0:
            loads[4].wait()
            loads[5].wait()
        for d in range(1, NY):
            arrive(rows(ffn_x, 128 * q + y_peer(NY - d) * 32, 32), yd_r.at[q, d], yd_s.at[q, d], at_dp(z, y_peer(d)))
        a = ffn_x[128 * q : 128 * q + 128, :]
        gu[128 * q : 128 * q + 128, 0:512] = dot(a, v_gate[...])
        gu[128 * q : 128 * q + 128, 512:1024] = dot(a, v_up[...])
        core_send[64 * q : 64 * q + 64, :] = gu[span(128 * q + (1 - c) * 64, 64), :]
        send(
            rows(core_send, 64 * q, 64), rows(core_recv, 64 * q, 64), co_s.at[q], co_r.at[q], {"tp": sibling}
        )

    def over_x(q):
        arrive(rows(core_recv, 64 * q, 64), co_r.at[q], co_s.at[q], {"tp": sibling})
        both = gu[span(128 * q + c * 64, 64), :] + core_recv[64 * q : 64 * q + 64, :]
        own_sum[64 * q : 64 * q + 64, :] = both
        x_send[64 * q : 64 * q + 64, :] = both.astype(BF16)
        for d in (2, 1, 3):
            to = x_peer(d)
            send(
                rows(x_send, 64 * q + to * 16, 16), rows(x_recv, 64 * q + x * 16, 16),
                xx_s.at[q, d], xx_r.at[q, d], {"tp": to * 2 + c},
            )

    def hidden(q):
        total = own_sum[span(64 * q + x * 16, 16), :]
        for d in range(1, NX):
            src = x_peer(NX - d)
            arrive(rows(x_recv, 64 * q + src * 16, 16), xx_r.at[q, d], xx_s.at[q, d], {"tp": src * 2 + c})
            total += x_recv[span(64 * q + src * 16, 16), :].astype(F32)
        gv, uv = total[:, 0:512], total[:, 512:1024]
        hid = gv / (1.0 + jnp.exp(-gv)) * uv
        place = 128 * q + c * 64 + x * 16
        h_all[span(place, 16), :] = hid.astype(BF16)
        for d in (4, 5, 3, 2, 6, 1, 7):
            send(
                rows(h_all, place, 16), rows(h_all, place, 16), hh_s.at[q, d], hh_r.at[q, d], {"tp": tp_peer(d)}
            )

    def second_ffn(q):
        if q == 0:
            loads[6].wait()
        for d in range(1, 8):
            src = tp_peer(8 - d)
            arrive(
                rows(h_all, 128 * q + src % 2 * 64 + src // 2 * 16, 16),
                hh_r.at[q, d], hh_s.at[q, d], {"tp": tp_peer(d)},
            )
        r_buf[128 * q : 128 * q + 128, :] = dot(h_all[128 * q : 128 * q + 128, :], v_down[...]).astype(BF16)
        for d in (2, 1, 3):
            to = y_peer(d)
            send(
                rows(r_buf, 128 * q + to * 32, 32), rows(p_buf, 128 * q + y * 32, 32),
                yr_s.at[q, d], yr_r.at[q, d], at_dp(z, to),
            )
        p_buf[span(128 * q + y * 32, 32), :] = r_buf[span(128 * q + y * 32, 32), :]

    def combine(q):
        for d in range(1, NY):
            arrive(rows(p_buf, 128 * q + y_peer(NY - d) * 32, 32), yr_r.at[q, d], yr_s.at[q, d], at_dp(z, y_peer(d)))
        meta = zbuf[64 * q : 64 * q + 64, WD:1024].astype(F32)
        col = iota((64, 128), 1)

        def column(at):
            return jnp.sum(jnp.where(col == at, meta, 0.0), axis=1, keepdims=True)

        base = iota((64, 1), 0) // 16 * 8 - 1
        s0, s1 = column(e0).astype(I32), column(e0 + 1).astype(I32)
        t0 = jnp.where(s0 > 0, s0 + base, -1)
        t1 = jnp.where(s1 > 0, s1 + base, -1)
        target = jnp.where(col < 64, t0, t1)
        gate = jnp.where(col < 64, column(e0 + 32), column(e0 + 33))
        mix = jnp.where(col % 32 == target, gate, 0.0).astype(BF16)
        part = dot(mix, p_buf[128 * q : 128 * q + 128, :])
        if q == 0:
            zs0[...] = part
            return
        zs[64 * q : 64 * q + 64, :] = part.astype(BF16)
        for d, at, there, size, i in passing:
            if there // 64 == q:
                dst = {64: rows(ra, 0, 64), 128: rows(rb, 0, 64), 192: rows(rc, 0, 32), 224: rows(rc, 32, 32)}[there]
                send(rows(zs, there, size), dst, rs_s.at[i], rs_r.at[i], z_peer(NZ - d))

    def gather():
        for (d, at, there, size, i), dst in zip(
            passing, (rows(ra, 0, 64), rows(rb, 0, 64), rows(rc, 0, 32), rows(rc, 32, 32))
        ):
            arrive(dst, rs_r.at[i], rs_s.at[i], z_peer(d))
        zs0[...] = zs0[...] + ra[...].astype(F32) + rb[...].astype(F32)
        zs0[0:32, :] = zs0[0:32, :] + rc[0:32, :].astype(F32)
        zs0[16:48, :] = zs0[16:48, :] + rc[32:64, :].astype(F32)
        far_send[...] = zs0[...].astype(BF16)
        for i, d in enumerate((8, 4, 12)):
            send(rows(far_send, 16 * ORDER.index(d), 16), rows(far_recv, 16 * i, 16), rs_s.at[i], rs_r.at[i], z_peer(d))

    def finish_moe():
        total = zs0[16:32, :]
        for i, d in enumerate((8, 4, 12)):
            arrive(rows(far_recv, 16 * i, 16), rs_r.at[i], rs_s.at[i], z_peer(d))
            total += far_recv[16 * i : 16 * i + 16, :].astype(F32)
        moe_out[...] = total.astype(BF16)

    def pack_pages():
        slot = page_slot[...]
        target, position = slot // 32, slot % 32
        r16 = iota((64, 32), 0)
        sel = jnp.where(r16 == 0, (position + 1).astype(F32), jnp.where(r16 == 1, prefill_scale[...].astype(F32), 0.0))
        spread = (iota((256, 32), 0) // 8 == iota((256, 32), 1)).astype(BF16)
        page_tail[:, 64:128] = dot(spread, sel.astype(BF16), 1, 1).astype(BF16)
        wide = jnp.broadcast_to(target.astype(F32), (16, 32)).astype(BF16)
        goal = dot(wide, spread, 1, 1)[0:1].astype(I32) * 8 + iota((1, 256), 1) % 8
        put = jnp.where(iota((512, 256), 0) == goal, 1.0, 0.0).astype(BF16)
        loads[1].wait()
        page_tail[:, 0:64] = v_pages[:, 512:576]
        pg_send[:, 0:512] = dot(put, v_pages[:, 0:512]).astype(BF16)
        pg_send[:, 512:640] = dot(put, page_tail[...]).astype(BF16)

    def send_pages(g):
        for k in range(4 * g, 4 * g + 4):
            d = (NZ - PAGE_ORDER[k]) % NZ
            to = lax.rem(z + d, NZ)
            if d:
                send(rows(pg_send, to * 32, 32), rows(pg_recv, 32 * k, 32), pz_s.at[k], pz_r.at[k], z_peer(d))
            else:
                pg_recv[32 * k : 32 * k + 32, :] = pg_send[span(to * 32, 32), :]

    def turn_pages(g):
        for k in range(4 * g, 4 * g + 4):
            if PAGE_ORDER[k]:
                arrive(rows(pg_recv, 32 * k, 32), pz_r.at[k], pz_s.at[k], z_peer(1))
        r = iota((128, 128), 0)
        src = r % 32 // 8 * 32 + r // 32 * 8 + r % 8
        turn = jnp.where(iota((128, 128), 1) == src, 1.0, 0.0).astype(BF16)
        pg_turn[128 * g : 128 * g + 128, :] = dot(turn, pg_recv[128 * g : 128 * g + 128, :]).astype(BF16)
        for d in (2, 1, 3):
            to = y_peer(d)
            send(
                rows(pg_turn, 128 * g + to * 32, 32), rows(pg_slots, 128 * g + y * 32, 32),
                py_s.at[g, d], py_r.at[g, d], at_dp(z, to),
            )
        pg_slots[span(128 * g + y * 32, 32), :] = pg_turn[span(128 * g + y * 32, 32), :]

    def place_pages():
        for g in range(4):
            for d in range(1, NY):
                src = y_peer(NY - d)
                arrive(rows(pg_slots, 128 * g + src * 32, 32), py_r.at[g, d], py_s.at[g, d], at_dp(z, src))
        pick = (iota((16, 128), 1) == 64).astype(BF16)
        position = dot(pick, pg_slots[:, 512:640], 1, 1)[0:1].astype(I32)
        goal = jnp.where(position > 0, (position - 1) * 8 + iota((1, 512), 1) % 8, -1)
        take = jnp.where(iota((256, 512), 0) == goal, 1.0, 0.0).astype(BF16)
        new_k[...] = dot(take, pg_slots[...]).astype(BF16)

    def score(r):
        if r == 0:
            loads[2].wait()
            loads[3].wait()
        pair, n = r // 2, r % 2
        if r < 2:
            rest = v_res[128 * r : 128 * r + 128, 512:576]
            value = v_res[128 * r : 128 * r + 128, 0:512]
            wide = jnp.broadcast_to(resident_scale[...].astype(F32), (16, 32)).astype(BF16)
            spread = (iota((128, 32), 0) // 8 + 16 * r == iota((128, 32), 1)).astype(BF16)
            scale = dot(spread, wide, 1, 1)[:, 0:1]
        else:
            rest = new_k[128 * n : 128 * n + 128, 512:576]
            value = new_k[128 * n : 128 * n + 128, 0:512]
            scale = new_k[128 * n : 128 * n + 128, 512:640].astype(F32)[:, 65:66]
        s = dot(value, v_q[r, 0:512, :]) + dot(rest, v_q[r, 512:576, :])
        row = iota((128, 128), 0)
        seen = row // 8 * 64 + tp * 8 + row % 8 < lengths[r]
        s = jnp.where(seen, s * (scale * FACTOR), MASKED)
        m = jnp.max(s, axis=0, keepdims=True)
        e = jnp.where(seen, jnp.exp(s - m), 0.0)
        l = jnp.sum(e, axis=0, keepdims=True)
        w = e * (scale / jnp.maximum(l, 1.0))
        part = dot(w.T.astype(BF16), value).astype(BF16)
        for i in range(8):
            at_send[256 * pair + 32 * i + 16 * n : 256 * pair + 32 * i + 16 * n + 16, :] = part[16 * i : 16 * i + 16, :]
        place = span(64 * pair + tp * 8, 8)
        row8 = iota((8, 128), 0)
        rest8 = jnp.zeros((8, 128), F32) if n == 0 else ml[place, :]
        ml[place, :] = jnp.where(row8 == n, m, jnp.where(row8 == n + 4, l, rest8))

    def send_attention(pair):
        for d in (4, 5, 3, 2, 6, 1, 7):
            to = tp_peer(d)
            place = rows(ml, 64 * pair + tp * 8, 8)
            send(place, place, ml_s.at[pair, d], ml_r.at[pair, d], {"tp": to})
            send(
                rows(at_send, 256 * pair + to * 32, 32), rows(at_recv, 256 * pair + tp * 32, 32),
                at_s.at[pair, d], at_r.at[pair, d], {"tp": to},
            )
        at_recv[span(256 * pair + tp * 32, 32), :] = at_send[span(256 * pair + tp * 32, 32), :]

    def finish_attention(pair):
        for d in range(1, 8):
            src = tp_peer(8 - d)
            arrive(rows(ml, 64 * pair + src * 8, 8), ml_r.at[pair, d], ml_s.at[pair, d], {"tp": src})
        m = [ml[64 * pair + 8 * i : 64 * pair + 8 * i + 4, :] for i in range(8)]
        l = [ml[64 * pair + 8 * i + 4 : 64 * pair + 8 * i + 8, :] for i in range(8)]
        highest = m[0]
        for i in range(1, 8):
            highest = jnp.maximum(highest, m[i])
        share = [l[i] * jnp.exp(m[i] - highest) for i in range(8)]
        total = share[0]
        for i in range(1, 8):
            total = total + share[i]
        inverse = 1.0 / total
        stacked = jnp.concatenate([share[i] * inverse for i in range(8)] + [jnp.zeros((96, 128), F32)], axis=0)
        wcol[...] = stacked.T
        mine = wcol[span(tp * 16, 16), :]
        for d in range(1, 8):
            src = tp_peer(8 - d)
            arrive(rows(at_recv, 256 * pair + src * 32, 32), at_r.at[pair, d], at_s.at[pair, d], {"tp": src})
        for n in range(2):
            out = jnp.zeros((16, 512), F32)
            for i in range(8):
                part = at_recv[256 * pair + 32 * i + 16 * n : 256 * pair + 32 * i + 16 * n + 16, :].astype(F32)
                out += part * mine[:, 4 * i + n : 4 * i + n + 1]
            att_out[2 * pair + n] = out.astype(BF16)

    stages = dict(
        enter=enter, far=far, far_wait=far_wait, near=near, near_wait=near_wait, dispatch=dispatch, first=first_ffn,
        over_x=over_x, hidden=hidden, second=second_ffn, combine=combine, gather=gather, finish_moe=finish_moe,
        pack=pack_pages, send_pages=send_pages, turn=turn_pages, place=place_pages, score=score,
        send_att=send_attention, finish_att=finish_attention,
    )
    for line in SCHEDULE:
        name, _, number = line.partition(" ")
        stages[name](*([int(number)] if number else []))
    for copy in started:
        copy.wait_send()


def on_device(
    queries, lengths, resident_pages, resident_scale, prefill_written_pages, prefill_scale,
    page_slot, tokens, expert_ids, gate_weights, gate_projection, up_weights, down_weights,
):
    vmem = pl.BlockSpec(memory_space=pltpu.VMEM)
    smem = pl.BlockSpec(memory_space=pltpu.SMEM)
    hbm = pl.BlockSpec(memory_space=pl.ANY)
    dma = pltpu.SemaphoreType.DMA
    return pl.pallas_call(
        kernel,
        out_shape=(
            jax.ShapeDtypeStruct((4, 16, 512), BF16),
            jax.ShapeDtypeStruct((16, WD), BF16),
        ),
        in_specs=[hbm, smem, hbm, vmem, hbm, vmem, vmem, hbm, vmem, vmem, hbm, hbm, hbm],
        out_specs=(vmem, vmem),
        scratch_shapes=[
            pltpu.VMEM((WD, 512), BF16),
            pltpu.VMEM((WD, 512), BF16),
            pltpu.VMEM((512, WD), BF16),
            pltpu.VMEM((4, 576, 128), BF16),
            pltpu.VMEM((256, 576), BF16),
            pltpu.VMEM((256, 576), BF16),
            pltpu.VMEM((256, 1024), BF16),
            pltpu.VMEM((256, WD), BF16),
            pltpu.VMEM((512, WD), BF16),
            pltpu.VMEM((512, 1024), F32),
            pltpu.VMEM((256, 1024), F32),
            pltpu.VMEM((256, 1024), F32),
            pltpu.VMEM((256, 1024), BF16),
            pltpu.VMEM((256, 1024), BF16),
            pltpu.VMEM((512, 512), BF16),
            pltpu.VMEM((512, WD), BF16),
            pltpu.VMEM((512, WD), BF16),
            pltpu.VMEM((64, WD), F32),
            pltpu.VMEM((256, WD), BF16),
            pltpu.VMEM((64, WD), BF16),
            pltpu.VMEM((64, WD), BF16),
            pltpu.VMEM((64, WD), BF16),
            pltpu.VMEM((64, WD), BF16),
            pltpu.VMEM((48, WD), BF16),
            pltpu.VMEM((256, 1024), F32),
            pltpu.VMEM((256, 128), BF16),
            pltpu.VMEM((512, 640), BF16),
            pltpu.VMEM((512, 640), BF16),
            pltpu.VMEM((512, 640), BF16),
            pltpu.VMEM((512, 640), BF16),
            pltpu.VMEM((256, 640), BF16),
            pltpu.VMEM((128, 128), F32),
            pltpu.VMEM((512, 512), BF16),
            pltpu.VMEM((512, 512), BF16),
            pltpu.VMEM((128, 128), F32),
            dma((7,)),
            dma((7,)), dma((7,)),
            dma((QN, 4)), dma((QN, 4)),
            dma((QN,)), dma((QN,)),
            dma((QN, 4)), dma((QN, 4)),
            dma((QN, 8)), dma((QN, 8)),
            dma((QN, 4)), dma((QN, 4)),
            dma((7,)), dma((7,)),
            dma((16,)), dma((16,)),
            dma((4, 4)), dma((4, 4)),
            dma((2, 8)), dma((2, 8)),
            dma((2, 8)), dma((2, 8)),
        ],
        compiler_params=pltpu.CompilerParams(
            collective_id=0, has_side_effects=True, vmem_limit_bytes=60 * 1024 * 1024
        ),
    )(
        queries.transpose(0, 2, 1),
        lengths,
        resident_pages.reshape(256, 576),
        resident_scale.reshape(1, 32),
        prefill_written_pages.reshape(256, 576),
        prefill_scale.reshape(1, 32),
        page_slot.reshape(1, 32),
        tokens,
        expert_ids.T,
        gate_weights.T,
        gate_projection.reshape(WD, 512),
        up_weights.reshape(WD, 512),
        down_weights.reshape(512, WD),
    )


def solution(mesh):
    placed = (
        P("dp", None, None), P("dp"), P("dp", "tp", None), P("dp"), P("dp", "tp", None), P("dp"),
        P("dp"), P("dp", None), P("dp", None), P("dp", None), P("dp", "tp", None),
        P("dp", "tp", None), P("dp", None, "tp"),
    )
    return jax.shard_map(
        on_device, mesh=mesh, in_specs=placed, out_specs=(P("dp", "tp", None), P("dp", "tp")),
        check_vma=False,
    )
```

time: 112 us -> 87.3 us (0.78)
  the two profiles are of different devices: /device:TPU:1 before, /device:TPU:2 now
where the time goes in v2:
time: 87.3 us; the launch traced here: 87.1 us
  Pallas kernels  84.4 us (97%)
  local copies, waits for them, and re-layouts  2.09 us (2%)
    pallas_call x1, Pallas kernels, on_device(): pl.pallas_call(kernel, out_shape=(jax.ShapeDtypeStruct((4, 16, 512), BF16...  84.4 us
    unnamed x4, local copies, waits for them, and re-layouts  2.09 us

profile of v2, /device:TPU:2, one launch (start us, length us, event | category | flops | bytes accessed | tf_op | source)
XLA Modules:
  0.0 87.1 jit_solution(902712916620550342)
XLA Ops:
  0.6 84.4 %shard_map.140 = (bf16[4,16,512]{2,1,0:T(8,128)(2,1)}, bf16[16,896]{1,0:T(8,128)(2,1)}) custom-call(bf16[4,576,128]{2,1,0:T(8,128)(2,1)} %bitcast.14, s32[4]{0:T(128)} %lengths.1, bf16[256,576]{1,0:T(8,128)(2,1)} %bitcast.15, bf16[1,32]{1,0:T(2,128)(2,1)} %bitcast.19, bf16[256,576]{1,0:T(8,128)(2,1)} %bitcast.16, bf16[1,32]{1,0:T(2,128)(2,1)} %bitcast.20, ...), custom_call_target="tpu_custom_call" | custom-call | tf_op jit(solution)/shard_map/pallas_call | solution.py:412
  85.0 0.0 copy-start
  85.0 1.5 %copy.17 = bf16[4,16,512]{2,1,0:T(8,128)(2,1)} copy(bf16[4,16,512]{2,1,0:T(8,128)(2,1)} %get-tuple-element.4) | data formatting | bytes 131072
  86.5 0.0 copy-done
  86.5 0.6 copy.18
Async XLA Ops:
  85.0 1.5 %copy-start = (bf16[16,896]{1,0:T(8,128)(2,1)S(1)}, bf16[16,896]{1,0:T(8,128)(2,1)}, u32[]{:S(2)}) copy-start(bf16[16,896]{1,0:T(8,128)(2,1)} %get-tuple-element.5) | copy-start | bytes 86020

commit v3 on v2

--- a/solution.py
+++ b/solution.py
@@ -38,9 +38,9 @@
     att_out, moe_out,
     v_gate, v_up, v_down, v_q, v_res, v_pages, zbuf, dsend, ffn_x, gu, core_send, core_recv, x_send, x_recv,
     h_all, r_buf, p_buf, zs0, zs, ra, rb, rc, far_send, far_recv, own_sum,
-    page_tail, pg_send, pg_recv, pg_turn, pg_slots, new_k, ml, at_send, at_recv, wcol,
+    page_tail, pg_send, pg_recv, tl_send, tl_recv, pg_turn, pg_slots, new_k, ml, at_send, at_recv, wcol,
     load_sem, zg_s, zg_r, yd_s, yd_r, co_s, co_r, xx_s, xx_r, hh_s, hh_r,
-    yr_s, yr_r, rs_s, rs_r, pz_s, pz_r, py_s, py_r, ml_s, ml_r, at_s, at_r,
+    yr_s, yr_r, rs_s, rs_r, pz_s, pz_r, pt_s, pt_r, py_s, py_r, ml_s, ml_r, at_s, at_r,
 ):
     tp = lax.axis_index("tp")
     dp = lax.axis_index("dp")
@@ -119,7 +119,12 @@
         gate_l += jnp.where(idv[:, k : k + 1] + 32 == lane, gwv[:, k : k + 1], 0.0)
     before = (iota((16, 16), 1) < iota((16, 16), 0)).astype(BF16)
     rank = dot(before, chosen.astype(BF16))
-    zbuf[16:32, WD:1024] = (chosen * (rank + 1.0) + gate_l).astype(BF16)
+    slot = page_slot[...]
+    r16 = iota((16, 32), 0)
+    sel = jnp.where(r16 == 0, (slot % 32 + 1).astype(F32), jnp.where(r16 == 1, prefill_scale[...].astype(F32), 0.0))
+    goes = (iota((128, 32), 0) - 64 == slot // 32).astype(BF16)
+    page_meta = dot(sel.astype(BF16), goes, 1, 1)
+    zbuf[16:32, WD:1024] = (chosen * (rank + 1.0) + gate_l + page_meta).astype(BF16)
 
     def enter():
         loads[0].wait()
@@ -269,19 +274,21 @@
         moe_out[...] = total.astype(BF16)
 
     def pack_pages():
-        slot = page_slot[...]
-        target, position = slot // 32, slot % 32
-        r16 = iota((64, 32), 0)
-        sel = jnp.where(r16 == 0, (position + 1).astype(F32), jnp.where(r16 == 1, prefill_scale[...].astype(F32), 0.0))
         spread = (iota((256, 32), 0) // 8 == iota((256, 32), 1)).astype(BF16)
-        page_tail[:, 64:128] = dot(spread, sel.astype(BF16), 1, 1).astype(BF16)
-        wide = jnp.broadcast_to(target.astype(F32), (16, 32)).astype(BF16)
+        wide = jnp.broadcast_to((slot // 32).astype(F32), (16, 32)).astype(BF16)
         goal = dot(wide, spread, 1, 1)[0:1].astype(I32) * 8 + iota((1, 256), 1) % 8
         put = jnp.where(iota((512, 256), 0) == goal, 1.0, 0.0).astype(BF16)
         loads[1].wait()
-        page_tail[:, 0:64] = v_pages[:, 512:576]
-        pg_send[:, 0:512] = dot(put, v_pages[:, 0:512]).astype(BF16)
-        pg_send[:, 512:640] = dot(put, page_tail[...]).astype(BF16)
+        pg_send[...] = dot(put, v_pages[:, 0:512]).astype(BF16)
+        page_tail[0, :, 0:64] = v_pages[:, 512:576]
+        page_tail[0, :, 64:128] = jnp.zeros((256, 64), BF16)
+        page_tail[1, :, 0:64] = jnp.zeros((256, 64), BF16)
+        page_tail[1, :, 64:128] = v_pages[:, 512:576]
+        row = iota((256, 256), 0)
+        first = row // 16 * 32 + row % 16
+        low = jnp.where(first == goal, 1.0, 0.0).astype(BF16)
+        high = jnp.where(first + 16 == goal, 1.0, 0.0).astype(BF16)
+        tl_send[...] = (dot(low, page_tail[0]) + dot(high, page_tail[1])).astype(BF16)
 
     def send_pages(g):
         for k in range(4 * g, 4 * g + 4):
@@ -289,17 +296,38 @@
             to = lax.rem(z + d, NZ)
             if d:
                 send(rows(pg_send, to * 32, 32), rows(pg_recv, 32 * k, 32), pz_s.at[k], pz_r.at[k], z_peer(d))
+                send(rows(tl_send, to * 16, 16), rows(tl_recv, 16 * k, 16), pt_s.at[k], pt_r.at[k], z_peer(d))
             else:
                 pg_recv[32 * k : 32 * k + 32, :] = pg_send[span(to * 32, 32), :]
+                tl_recv[16 * k : 16 * k + 16, :] = tl_send[span(to * 16, 16), :]
 
     def turn_pages(g):
         for k in range(4 * g, 4 * g + 4):
             if PAGE_ORDER[k]:
                 arrive(rows(pg_recv, 32 * k, 32), pz_r.at[k], pz_s.at[k], z_peer(1))
+                arrive(rows(tl_recv, 16 * k, 16), pt_r.at[k], pt_s.at[k], z_peer(1))
         r = iota((128, 128), 0)
         src = r % 32 // 8 * 32 + r // 32 * 8 + r % 8
         turn = jnp.where(iota((128, 128), 1) == src, 1.0, 0.0).astype(BF16)
-        pg_turn[128 * g : 128 * g + 128, :] = dot(turn, pg_recv[128 * g : 128 * g + 128, :]).astype(BF16)
+        pg_turn[128 * g : 128 * g + 128, 0:512] = dot(turn, pg_recv[128 * g : 128 * g + 128, :]).astype(BF16)
+        r = iota((128, 64), 0)
+        src = r % 32 // 8 * 16 + r // 32 % 2 * 8 + r % 8
+        turn = jnp.where(iota((128, 64), 1) == src, 1.0, 0.0).astype(BF16)
+        tail = dot(turn, tl_recv[64 * g : 64 * g + 64, :])
+        swapped = jnp.concatenate([tail[:, 64:128], tail[:, 0:64]], axis=1)
+        r, lane = iota((128, 128), 0), iota((128, 128), 1)
+        place, scale = jnp.zeros((128, 128), F32), jnp.zeros((128, 128), F32)
+        for k in range(4):
+            at = 16 * ORDER.index(PAGE_ORDER[4 * g + k])
+            meta = zbuf[at : at + 16, WD:1024].astype(F32)
+            place = jnp.where(r % 32 // 8 == k, meta[0:1], place)
+            scale = jnp.where(r % 32 // 8 == k, meta[1:2], scale)
+        hit = lane == 64 + 4 * z + r // 32
+        place = jnp.sum(jnp.where(hit, place, 0.0), axis=1, keepdims=True)
+        scale = jnp.sum(jnp.where(hit, scale, 0.0), axis=1, keepdims=True)
+        tail = jnp.where(lane < 64, jnp.where(r < 64, tail, swapped), 0.0)
+        tail = jnp.where(lane == 64, place, jnp.where(lane == 65, scale, tail))
+        pg_turn[128 * g : 128 * g + 128, 512:640] = tail.astype(BF16)
         for d in (2, 1, 3):
             to = y_peer(d)
             send(
@@ -443,9 +471,11 @@
             pltpu.VMEM((64, WD), BF16),
             pltpu.VMEM((48, WD), BF16),
             pltpu.VMEM((256, 1024), F32),
+            pltpu.VMEM((2, 256, 128), BF16),
+            pltpu.VMEM((512, 512), BF16),
+            pltpu.VMEM((512, 512), BF16),
             pltpu.VMEM((256, 128), BF16),
-            pltpu.VMEM((512, 640), BF16),
-            pltpu.VMEM((512, 640), BF16),
+            pltpu.VMEM((256, 128), BF16),
             pltpu.VMEM((512, 640), BF16),
             pltpu.VMEM((512, 640), BF16),
             pltpu.VMEM((256, 640), BF16),
@@ -461,6 +491,7 @@
             dma((QN, 8)), dma((QN, 8)),
             dma((QN, 4)), dma((QN, 4)),
             dma((7,)), dma((7,)),
+            dma((16,)), dma((16,)),
             dma((16,)), dma((16,)),
             dma((4, 4)), dma((4, 4)),
             dma((2, 8)), dma((2, 8)),

time: 87.3 us -> 85.6 us (0.981)
  the two profiles are of different devices: /device:TPU:2 before, /device:TPU:16 now
where the time goes in v3:
time: 85.6 us; the launch traced here: 85.4 us
  Pallas kernels  82.7 us (97%)
  local copies, waits for them, and re-layouts  2.09 us (2%)
    pallas_call x1, Pallas kernels, on_device(): pl.pallas_call(kernel, out_shape=(jax.ShapeDtypeStruct((4, 16, 512), BF16...  82.7 us
    unnamed x4, local copies, waits for them, and re-layouts  2.09 us

profile of v3, /device:TPU:16, one launch (start us, length us, event | category | flops | bytes accessed | tf_op | source)
XLA Modules:
  0.0 85.4 jit_solution(15583515923250660015)
XLA Ops:
  0.6 82.7 %shard_map.140 = (bf16[4,16,512]{2,1,0:T(8,128)(2,1)}, bf16[16,896]{1,0:T(8,128)(2,1)}) custom-call(bf16[4,576,128]{2,1,0:T(8,128)(2,1)} %bitcast.14, s32[4]{0:T(128)} %lengths.1, bf16[256,576]{1,0:T(8,128)(2,1)} %bitcast.15, bf16[1,32]{1,0:T(2,128)(2,1)} %bitcast.19, bf16[256,576]{1,0:T(8,128)(2,1)} %bitcast.16, bf16[1,32]{1,0:T(2,128)(2,1)} %bitcast.20, ...), custom_call_target="tpu_custom_call" | custom-call | tf_op jit(solution)/shard_map/pallas_call | solution.py:440
  83.3 0.0 copy-start
  83.3 1.5 %copy.17 = bf16[4,16,512]{2,1,0:T(8,128)(2,1)} copy(bf16[4,16,512]{2,1,0:T(8,128)(2,1)} %get-tuple-element.4) | data formatting | bytes 131072
  84.8 0.0 copy-done
  84.8 0.6 copy.18
Async XLA Ops:
  83.3 1.5 %copy-start = (bf16[16,896]{1,0:T(8,128)(2,1)S(1)}, bf16[16,896]{1,0:T(8,128)(2,1)}, u32[]{:S(2)}) copy-start(bf16[16,896]{1,0:T(8,128)(2,1)} %get-tuple-element.5) | copy-start | bytes 86020

commit v4 on v2

--- a/solution.py
+++ b/solution.py
@@ -10,12 +10,12 @@
 FACTOR = 192.0 ** (-0.5)
 MASKED = -1e30
 SCHEDULE = [
-    "pack", "score 0", "score 1", "enter", "far", "send_att 0", "far_wait", "near", "dispatch 0",
+    "pack", "score 0", "score 1", "enter", "far", "pages_y", "send_att 0", "far_wait", "near", "dispatch 0",
     "near_wait 1", "dispatch 1", "first 0", "near_wait 2", "dispatch 2", "over_x 0", "near_wait 3", "dispatch 3",
-    "send_pages 0", "send_pages 1", "send_pages 2", "send_pages 3", "first 1", "hidden 0", "over_x 1", "first 2",
+    "turn", "send_pages 0", "send_pages 1", "send_pages 2", "send_pages 3", "first 1", "hidden 0", "over_x 1", "first 2",
     "second 0", "hidden 1", "over_x 2", "first 3", "second 1", "hidden 2", "over_x 3", "combine 0", "second 2",
-    "hidden 3", "combine 1", "turn 0", "second 3", "combine 2", "turn 1", "combine 3", "turn 2", "finish_att 0",
-    "turn 3", "place", "gather", "score 2", "score 3", "send_att 1", "finish_moe", "finish_att 1",
+    "hidden 3", "combine 1", "second 3", "combine 2", "combine 3", "finish_att 0", "unpack 0", "unpack 1", "unpack 2",
+    "unpack 3", "place", "score 2", "score 3", "send_att 1", "gather", "finish_att 1", "finish_moe",
 ]
 NZ, NY, NX = 16, 4, 4
 QN = 4
@@ -38,9 +38,9 @@
     att_out, moe_out,
     v_gate, v_up, v_down, v_q, v_res, v_pages, zbuf, dsend, ffn_x, gu, core_send, core_recv, x_send, x_recv,
     h_all, r_buf, p_buf, zs0, zs, ra, rb, rc, far_send, far_recv, own_sum,
-    page_tail, pg_send, pg_recv, pg_turn, pg_slots, new_k, ml, at_send, at_recv, wcol,
+    page_tail, pg_send, pg_y, pg_z, tl_z, mt_z, tl_recv, mt_recv, pg_slots, new_k, ml, at_send, at_recv, wcol,
     load_sem, zg_s, zg_r, yd_s, yd_r, co_s, co_r, xx_s, xx_r, hh_s, hh_r,
-    yr_s, yr_r, rs_s, rs_r, pz_s, pz_r, py_s, py_r, ml_s, ml_r, at_s, at_r,
+    yr_s, yr_r, rs_s, rs_r, pz_s, pz_r, pt_s, pt_r, pm_s, pm_r, py_s, py_r, ml_s, ml_r, at_s, at_r,
 ):
     tp = lax.axis_index("tp")
     dp = lax.axis_index("dp")
@@ -270,12 +270,15 @@
 
     def pack_pages():
         slot = page_slot[...]
-        target, position = slot // 32, slot % 32
-        r16 = iota((64, 32), 0)
-        sel = jnp.where(r16 == 0, (position + 1).astype(F32), jnp.where(r16 == 1, prefill_scale[...].astype(F32), 0.0))
+        r64 = iota((64, 32), 0)
+        sel = jnp.where(
+            r64 == 0, (slot % 32 + 1).astype(F32), jnp.where(r64 == 1, prefill_scale[...].astype(F32), 0.0)
+        )
         spread = (iota((256, 32), 0) // 8 == iota((256, 32), 1)).astype(BF16)
         page_tail[:, 64:128] = dot(spread, sel.astype(BF16), 1, 1).astype(BF16)
-        wide = jnp.broadcast_to(target.astype(F32), (16, 32)).astype(BF16)
+        target = slot // 32
+        where = target % 4 * 16 + target // 4
+        wide = jnp.broadcast_to(where.astype(F32), (16, 32)).astype(BF16)
         goal = dot(wide, spread, 1, 1)[0:1].astype(I32) * 8 + iota((1, 256), 1) % 8
         put = jnp.where(iota((512, 256), 0) == goal, 1.0, 0.0).astype(BF16)
         loads[1].wait()
@@ -283,36 +286,70 @@
         pg_send[:, 0:512] = dot(put, v_pages[:, 0:512]).astype(BF16)
         pg_send[:, 512:640] = dot(put, page_tail[...]).astype(BF16)
 
+    def pages_y():
+        for d in (2, 1, 3):
+            to = y_peer(d)
+            send(rows(pg_send, to * 128, 128), rows(pg_y, y * 128, 128), py_s.at[d], py_r.at[d], at_dp(z, to))
+        pg_y[span(y * 128, 128), :] = pg_send[span(y * 128, 128), :]
+
+    def turn_pages():
+        for d in range(1, NY):
+            arrive(rows(pg_y, y_peer(NY - d) * 128, 128), py_r.at[d], py_s.at[d], at_dp(z, y_peer(d)))
+        r, col = iota((512, 512), 0), iota((512, 512), 1)
+        turn = jnp.where(col == r % 32 // 8 * 128 + r // 32 * 8 + r % 8, 1.0, 0.0).astype(BF16)
+        pg_z[...] = dot(turn, pg_y[:, 0:512]).astype(BF16)
+        tail = pg_y[:, 512:640]
+        lane = iota((512, 128), 1)
+        columns = jnp.where(lane < 64, tail.astype(F32), 0.0)
+        swapped = jnp.concatenate([columns[:, 64:128], columns[:, 0:64]], axis=1)
+        r, col = iota((256, 512), 0), iota((256, 512), 1)
+        src = r % 16 // 8 * 128 + r // 16 * 8 + r % 8
+        low = jnp.where(col == src, 1.0, 0.0).astype(BF16)
+        high = jnp.where(col == src + 256, 1.0, 0.0).astype(BF16)
+        tl_z[...] = (dot(low, columns.astype(BF16)) + dot(high, swapped.astype(BF16))).astype(BF16)
+        r, lane, col = iota((16, 128), 0), iota((16, 128), 1), iota((16, 512), 1)
+        meta = jnp.zeros((16, 128), F32)
+        for k in range(4):
+            first = jnp.where(col == k * 128 + iota((16, 512), 0) * 8, 1.0, 0.0).astype(BF16)
+            got = dot(first, tail)
+            meta = jnp.where(lane == k, got[:, 64:65], jnp.where(lane == k + 8, got[:, 65:66], meta))
+        for k in range(NZ):
+            mt_z[k] = meta[k : k + 1, :]
+
     def send_pages(g):
         for k in range(4 * g, 4 * g + 4):
             d = (NZ - PAGE_ORDER[k]) % NZ
             to = lax.rem(z + d, NZ)
             if d:
-                send(rows(pg_send, to * 32, 32), rows(pg_recv, 32 * k, 32), pz_s.at[k], pz_r.at[k], z_peer(d))
+                send(rows(pg_z, to * 32, 32), pg_slots.at[pl.ds(32 * k, 32), pl.ds(0, 512)], pz_s.at[k], pz_r.at[k], z_peer(d))
+                send(rows(tl_z, to * 16, 16), rows(tl_recv, 16 * k, 16), pt_s.at[k], pt_r.at[k], z_peer(d))
+                send(mt_z.at[to], mt_recv.at[k], pm_s.at[k], pm_r.at[k], z_peer(d))
             else:
-                pg_recv[32 * k : 32 * k + 32, :] = pg_send[span(to * 32, 32), :]
-
-    def turn_pages(g):
+                pg_slots[32 * k : 32 * k + 32, 0:512] = pg_z[span(to * 32, 32), :]
+                tl_recv[16 * k : 16 * k + 16, :] = tl_z[span(to * 16, 16), :]
+                mt_recv[k] = mt_z[to]
+
+    def unpack(g):
         for k in range(4 * g, 4 * g + 4):
             if PAGE_ORDER[k]:
-                arrive(rows(pg_recv, 32 * k, 32), pz_r.at[k], pz_s.at[k], z_peer(1))
-        r = iota((128, 128), 0)
-        src = r % 32 // 8 * 32 + r // 32 * 8 + r % 8
-        turn = jnp.where(iota((128, 128), 1) == src, 1.0, 0.0).astype(BF16)
-        pg_turn[128 * g : 128 * g + 128, :] = dot(turn, pg_recv[128 * g : 128 * g + 128, :]).astype(BF16)
-        for d in (2, 1, 3):
-            to = y_peer(d)
-            send(
-                rows(pg_turn, 128 * g + to * 32, 32), rows(pg_slots, 128 * g + y * 32, 32),
-                py_s.at[g, d], py_r.at[g, d], at_dp(z, to),
-            )
-        pg_slots[span(128 * g + y * 32, 32), :] = pg_turn[span(128 * g + y * 32, 32), :]
+                arrive(pg_slots.at[pl.ds(32 * k, 32), pl.ds(0, 512)], pz_r.at[k], pz_s.at[k], z_peer(1))
+                arrive(rows(tl_recv, 16 * k, 16), pt_r.at[k], pt_s.at[k], z_peer(1))
+                arrive(mt_recv.at[k], pm_r.at[k], pm_s.at[k], z_peer(1))
+        r, col = iota((128, 64), 0), iota((128, 64), 1)
+        pick = jnp.where(col == r // 32 * 16 + r % 16, 1.0, 0.0).astype(BF16)
+        tail = dot(pick, tl_recv[64 * g : 64 * g + 64, :])
+        swapped = jnp.concatenate([tail[:, 64:128], tail[:, 0:64]], axis=1)
+        r, lane = iota((128, 128), 0), iota((128, 128), 1)
+        meta = jnp.zeros((128, 128), F32)
+        for k in range(4):
+            meta = jnp.where(r // 32 == k, mt_recv[4 * g + k], meta)
+        place = jnp.sum(jnp.where(lane == r % 32 // 8, meta, 0.0), axis=1, keepdims=True)
+        scale = jnp.sum(jnp.where(lane == r % 32 // 8 + 8, meta, 0.0), axis=1, keepdims=True)
+        tail = jnp.where(lane < 64, jnp.where(r % 32 < 16, tail, swapped), 0.0)
+        tail = jnp.where(lane == 64, place, jnp.where(lane == 65, scale, tail))
+        pg_slots[128 * g : 128 * g + 128, 512:640] = tail.astype(BF16)
 
     def place_pages():
-        for g in range(4):
-            for d in range(1, NY):
-                src = y_peer(NY - d)
-                arrive(rows(pg_slots, 128 * g + src * 32, 32), py_r.at[g, d], py_s.at[g, d], at_dp(z, src))
         pick = (iota((16, 128), 1) == 64).astype(BF16)
         position = dot(pick, pg_slots[:, 512:640], 1, 1)[0:1].astype(I32)
         goal = jnp.where(position > 0, (position - 1) * 8 + iota((1, 512), 1) % 8, -1)
@@ -391,7 +428,7 @@
     stages = dict(
         enter=enter, far=far, far_wait=far_wait, near=near, near_wait=near_wait, dispatch=dispatch, first=first_ffn,
         over_x=over_x, hidden=hidden, second=second_ffn, combine=combine, gather=gather, finish_moe=finish_moe,
-        pack=pack_pages, send_pages=send_pages, turn=turn_pages, place=place_pages, score=score,
+        pack=pack_pages, send_pages=send_pages, pages_y=pages_y, turn=turn_pages, unpack=unpack, place=place_pages, score=score,
         send_att=send_attention, finish_att=finish_attention,
     )
     for line in SCHEDULE:
@@ -446,7 +483,11 @@
             pltpu.VMEM((256, 128), BF16),
             pltpu.VMEM((512, 640), BF16),
             pltpu.VMEM((512, 640), BF16),
-            pltpu.VMEM((512, 640), BF16),
+            pltpu.VMEM((512, 512), BF16),
+            pltpu.VMEM((256, 128), BF16),
+            pltpu.VMEM((16, 1, 128), F32),
+            pltpu.VMEM((256, 128), BF16),
+            pltpu.VMEM((16, 1, 128), F32),
             pltpu.VMEM((512, 640), BF16),
             pltpu.VMEM((256, 640), BF16),
             pltpu.VMEM((128, 128), F32),
@@ -462,7 +503,9 @@
             dma((QN, 4)), dma((QN, 4)),
             dma((7,)), dma((7,)),
             dma((16,)), dma((16,)),
-            dma((4, 4)), dma((4, 4)),
+            dma((16,)), dma((16,)),
+            dma((16,)), dma((16,)),
+            dma((4,)), dma((4,)),
             dma((2, 8)), dma((2, 8)),
             dma((2, 8)), dma((2, 8)),
         ],

time: 87.3 us -> 83.3 us (0.954)
  the two profiles are of different devices: /device:TPU:2 before, /device:TPU:1 now
where the time goes in v4:
time: 83.3 us; the launch traced here: 83.1 us
  Pallas kernels  80.3 us (96%)
  local copies, waits for them, and re-layouts  2.09 us (3%)
    pallas_call x1, Pallas kernels, on_device(): pl.pallas_call(kernel, out_shape=(jax.ShapeDtypeStruct((4, 16, 512), BF16...  80.3 us
    unnamed x4, local copies, waits for them, and re-layouts  2.09 us

profile of v4, /device:TPU:1, one launch (start us, length us, event | category | flops | bytes accessed | tf_op | source)
XLA Modules:
  0.0 83.1 jit_solution(3173741174490885277)
XLA Ops:
  0.6 80.3 %shard_map.140 = (bf16[4,16,512]{2,1,0:T(8,128)(2,1)}, bf16[16,896]{1,0:T(8,128)(2,1)}) custom-call(bf16[4,576,128]{2,1,0:T(8,128)(2,1)} %bitcast.14, s32[4]{0:T(128)} %lengths.1, bf16[256,576]{1,0:T(8,128)(2,1)} %bitcast.15, bf16[1,32]{1,0:T(2,128)(2,1)} %bitcast.19, bf16[256,576]{1,0:T(8,128)(2,1)} %bitcast.16, bf16[1,32]{1,0:T(2,128)(2,1)} %bitcast.20, ...), custom_call_target="tpu_custom_call" | custom-call | tf_op jit(solution)/shard_map/pallas_call | solution.py:449
  81.0 0.0 copy-start
  81.0 1.5 %copy.17 = bf16[4,16,512]{2,1,0:T(8,128)(2,1)} copy(bf16[4,16,512]{2,1,0:T(8,128)(2,1)} %get-tuple-element.4) | data formatting | bytes 131072
  82.5 0.0 copy-done
  82.5 0.6 copy.18
Async XLA Ops:
  81.0 1.5 %copy-start = (bf16[16,896]{1,0:T(8,128)(2,1)S(1)}, bf16[16,896]{1,0:T(8,128)(2,1)}, u32[]{:S(2)}) copy-start(bf16[16,896]{1,0:T(8,128)(2,1)} %get-tuple-element.5) | copy-start | bytes 86020
